TPU v7x, 512 devices: a whole 4x4x16 slice. The times are simulated.
512 devices in a mesh: vocab: 64 (over z, x), tok: 8 (over y, core).
Axes of the slice: x: 4, y: 4, z: 16, core: 2. Of those that a mesh axis runs over, the one named last changes fastest.
Arguments:
- target_logits: bfloat16 [1024, 131072], P('tok', 'vocab'), may hold values from -250 to 250
- draft_hidden: bfloat16 [2, 1024, 4096], P(None, 'tok', 'vocab'), may hold values from -210 to 210
- draft_head: bfloat16 [32768, 4096], P('vocab'), may hold values from -0.375 to 0.375
- block_map: int32 [256], replicated, may hold values from 0 to 1023, as said below
Outputs:
- grad_hidden: bfloat16 [2, 1024, 4096], P(None, 'tok', 'vocab')
- per_token_loss: float32 [2, 1024], P(None, ('tok', 'vocab'))
Inputs may be any that keep to these rules, and one draw needn't show every extreme that they name: block_map names 256 different target blocks; at most 8 of them lie among the 16 blocks of one vocab device, and exactly 8 on some device.
All inputs are finite; a program needn't handle non-finite values.
Results may differ from a plain program's by a relative error of at most 0.004.
The roundings to bfloat16 on the way count: a program that leaves them out, or rounds other values in their place, can miss the bound.
Values may be sent and summed in bfloat16 or wider, within the bound.
A program may use at most 64 MiB of HBM per device.

v0:
```python
import jax
import jax.numpy as jnp
from jax import lax
from jax.sharding import PartitionSpec as P

BLK = 128
TBLK_DEV = 16
SEL_MAX = 8


loss_scale = 64.0


def from_behind(value, axis, by):
    size = lax.axis_size(axis)
    pairs = [(i, i + by) for i in range(size) if 0 <= i + by < size]
    return lax.ppermute(value, axis, pairs)


def joined(part, axis, combine):
    gathered = jax.tree.map(lambda a: lax.all_gather(a, axis), part)

    def take(source):
        return jax.tree.map(lambda a: lax.dynamic_index_in_dim(a, source, 0, False), gathered)

    return lax.fori_loop(
        1, lax.axis_size(axis), lambda source, state: combine(state, take(source)), take(0)
    )


def merge_pairs(first, second):
    merged = []
    for index in range(0, len(first), 2):
        highest = jnp.maximum(first[index], second[index])
        summed = first[index + 1] * jnp.exp(first[index] - highest) + second[index + 1] * jnp.exp(
            second[index] - highest
        )
        merged.append(highest)
        merged.append(summed)
    return tuple(merged)


def softmax_stats(values):
    highest = jnp.max(values, axis=-1)
    return (highest, jnp.sum(jnp.exp(values - highest[..., None]), axis=-1))


def on_device(target_logits, draft_hidden, draft_head, block_map):
    vocab_count = lax.axis_size("vocab")
    vocab_rank = lax.axis_index("vocab")
    tok_rank = lax.axis_index("tok")
    tok_rows = target_logits.shape[0]
    steps = draft_hidden.shape[0]
    width_part = draft_hidden.shape[2]
    draft_cols = draft_head.shape[0]
    share = tok_rows // vocab_count
    draft_blocks = block_map.shape[0]
    owner = block_map // TBLK_DEV
    local = block_map % TBLK_DEV
    same_owner = owner[:, None] == owner[None, :]
    before = local[None, :] < local[:, None]
    rank = jnp.sum((same_owner & before).astype(jnp.int32), axis=1)
    slot_ids = jnp.arange(SEL_MAX, dtype=jnp.int32)
    hits = (owner[None, :] == vocab_rank) & (rank[None, :] == slot_ids[:, None])
    slot_block = jnp.sum(jnp.where(hits, local[None, :], 0), axis=1)
    compact = jnp.take(target_logits.reshape(tok_rows, TBLK_DEV, BLK), slot_block, axis=1)
    received = lax.all_to_all(
        compact.reshape(tok_rows, 1, SEL_MAX * BLK),
        "vocab",
        split_axis=0,
        concat_axis=1,
        tiled=True,
    )
    flat = received.reshape(share, vocab_count * SEL_MAX, BLK)
    picked = jnp.take(flat, owner * SEL_MAX + rank, axis=1).reshape(share, draft_blocks * BLK)
    target_vals = target_logits.astype(jnp.float32)
    target_top, target_sum = softmax_stats(target_vals)
    tail = draft_hidden[:, tok_rows - (steps - 1) :, :]
    earlier = from_behind(tail, "tok", 1)
    shifted = [draft_hidden[0]]
    step_index = 1
    shifted.append(
        jnp.concatenate(
            [
                earlier[step_index, steps - 1 - step_index :],
                draft_hidden[step_index, : tok_rows - step_index],
            ],
            axis=0,
        )
    )
    shifted = jnp.stack(shifted)
    columns = draft_head
    summed = jnp.einsum(
        "std,cd->stc",
        lax.all_gather(shifted, "vocab", axis=2, tiled=True),
        columns,
        preferred_element_type=jnp.float32,
    )
    logits_half = lax.optimization_barrier(summed.astype(jnp.bfloat16))
    step_ids = jnp.arange(steps, dtype=jnp.int32)
    mine_blocks = lax.all_to_all(
        picked.reshape(share, vocab_count, draft_cols),
        "vocab",
        split_axis=1,
        concat_axis=0,
        tiled=True,
    )
    mine_vals = mine_blocks.reshape(tok_rows, draft_cols).astype(jnp.float32)
    logits = logits_half.astype(jnp.float32)
    kept_top, kept_sum = softmax_stats(mine_vals)
    draft_top, draft_sum = softmax_stats(logits)
    merged = joined(
        (target_top, target_sum, kept_top, kept_sum, draft_top, draft_sum), "vocab", merge_pairs
    )
    target_lse = merged[0] + jnp.log(merged[1])
    kept_lse = merged[2] + jnp.log(merged[3])
    draft_lse = merged[4] + jnp.log(merged[5])
    target_mass = jnp.exp(kept_lse - target_lse)
    target_probs = jnp.exp(mine_vals - target_lse[:, None])
    rows_here = tok_rank * tok_rows + jnp.arange(tok_rows, dtype=jnp.int32)
    keep = (rows_here[None, :] >= step_ids[:, None]).astype(jnp.float32)
    partial_loss = keep * jnp.sum(target_probs[None] * (draft_lse[..., None] - logits), axis=-1)
    token_loss = lax.psum_scatter(partial_loss, "vocab", scatter_dimension=1, tiled=True)
    returned = (
        loss_scale
        * keep[..., None]
        * (target_mass[None, :, None] * jnp.exp(logits - draft_lse[..., None]) - target_probs[None])
    ).astype(jnp.bfloat16)
    columns = draft_head
    grand = lax.psum(
        jnp.einsum("cd,stc->dst", columns, returned, preferred_element_type=jnp.float32), "vocab"
    )
    owned = lax.dynamic_slice_in_dim(grand, vocab_rank * width_part, width_part, 0)
    state_grads = jnp.transpose(owned, (1, 2, 0))
    heads = state_grads[:, : steps - 1, :]
    later = from_behind(heads, "tok", -1)
    pieces = [state_grads[0]]
    step_index = 1
    pieces.append(
        jnp.concatenate(
            [state_grads[step_index, step_index:], later[step_index, :step_index]], axis=0
        )
    )
    return (jnp.stack(pieces).astype(jnp.bfloat16), token_loss)


def solution(mesh):
    return jax.shard_map(
        on_device,
        mesh=mesh,
        in_specs=(P("tok", "vocab"), P(None, "tok", "vocab"), P("vocab", None), P()),
        out_specs=(P(None, "tok", "vocab"), P(None, ("tok", "vocab"))),
        check_vma=False,
    )
```

profile of v0, /device:TPU:1, one launch (start us, length us, event | category | flops | bytes accessed | tf_op | source)
XLA Modules:
  0.0 881.7 jit_solution(8920158904762778084)
XLA Ops:
  7.2 0.9 slice.34
  8.1 4.6 collective-permute-start
  12.7 0.7 slice_bitcast_fusion.2
  13.4 0.7 broadcast_compare_fusion
  14.1 0.7 slice.33
  14.9 2.1 collective-permute-done
  17.1 0.6 pad_maximum_fusion.1
  17.7 0.7 and_select_fusion
  18.4 1.3 copy.39
  19.7 0.3 copy.40
  20.0 0.2 convert_reduce_fusion
  20.4 0.6 gather_fusion
  21.0 0.2 copy.41
  21.2 0.2 bitcast_select_fusion
  21.4 0.5 broadcast.158
  22.0 0.8 reduce.6
  22.8 0.1 copy.63
  22.9 0.8 reshape.246
  23.8 16.2 %all-to-all-start = ((bf16[64,2,1024]{2,1,0:T(2,128)(2,1)}), bf16[64,2,1024]{2,1,0:T(2,128)(2,1)S(1)}, u32[]{:S(2)}, u32[]{:S(2)}) async-start(bf16[64,2,1024]{2,1,0:T(2,128)(2,1)} %reshape.246), calls=%async_computation | async-start | bytes 524288 | tf_op jit(solution)/shard_map/all_to_all | solution.py:67
  40.3 0.2 reduce_max.54
  40.4 1.3 dynamic-slice
  42.3 0.3 exponential_reduce_fusion
  42.6 72.2 %all-gather.5 = f32[64,1,128]{2,1,0:T(1,128)S(1)} all-gather(f32[1,1,128]{2,1,0:T(1,128)S(1)} %bitcast.132), channel_id=3, replica_groups=mesh['vocab'=64,'tok'=8] {'vocab'}, dimensions={0}, use_global_device_ids=true | all-gather | bytes 33280 | tf_op jit(solution)/shard_map/all_gather | solution.py:21
  114.7 61.8 %all-gather.4 = f32[64,1,128]{2,1,0:T(1,128)S(1)} all-gather(f32[1,1,128]{2,1,0:T(1,128)S(1)} %get-tuple-element.378), channel_id=2, replica_groups=mesh['vocab'=64,'tok'=8] {'vocab'}, dimensions={0}, use_global_device_ids=true | all-gather | bytes 33280 | tf_op jit(solution)/shard_map/all_gather | solution.py:21
  176.5 0.2 reshape.247
  176.8 1.5 reduce.5
  178.4 0.9 gather_fusion.1
  179.5 0.8 copy.46
  180.3 8.6 all-to-all-start.1
  188.9 15.0 %all-to-all-done.1 = bf16[2,64,512]{2,0,1:T(2,128)(2,1)S(1)} async-done(((bf16[2,64,512]{2,0,1:T(2,128)(2,1)}), bf16[2,64,512]{2,0,1:T(2,128)(2,1)S(1)}, u32[]{:S(2)}, u32[]{:S(2)}) %all-to-all-start.1) | async-done | bytes 131104 | tf_op jit(solution)/shard_map/all_to_all | solution.py:101
  203.9 0.2 bitcast_reduce_fusion
  204.1 0.1 reshape.219
  204.2 0.3 exponential_reduce_fusion.1
  204.8 0.2 reshape.185
  205.0 54.7 %all-gather.7 = f32[64,1,128]{2,1,0:T(1,128)S(1)} all-gather(f32[1,1,128]{2,1,0:T(1,128)S(1)} %reshape.221), channel_id=1, replica_groups=mesh['vocab'=64,'tok'=8] {'vocab'}, dimensions={0}, use_global_device_ids=true | all-gather | bytes 33280 | tf_op jit(solution)/shard_map/all_gather | solution.py:21
  259.7 55.4 %all-gather.6 = f32[64,1,128]{2,1,0:T(1,128)S(1)} all-gather(f32[1,1,128]{2,1,0:T(1,128)S(1)} %reshape.219), channel_id=1, replica_groups=mesh['vocab'=64,'tok'=8] {'vocab'}, dimensions={0}, use_global_device_ids=true | all-gather | bytes 33280 | tf_op jit(solution)/shard_map/all_gather | solution.py:21
  315.1 4.1 fusion.18
  319.3 0.2 fusion.22
  319.6 61.3 %all-gather.9 = f32[64,2,128]{2,1,0:T(2,128)S(1)} all-gather(f32[1,2,128]{2,1,0:T(2,128)S(1)} %bitcast.131), channel_id=5, replica_groups=mesh['vocab'=64,'tok'=8] {'vocab'}, dimensions={0}, use_global_device_ids=true | all-gather | bytes 66560 | tf_op jit(solution)/shard_map/all_gather | solution.py:21
  380.9 61.7 %all-gather.8 = f32[64,2,128]{2,1,0:T(2,128)S(1)} all-gather(f32[1,2,128]{2,1,0:T(2,128)S(1)} %get-tuple-element.376), channel_id=4, replica_groups=mesh['vocab'=64,'tok'=8] {'vocab'}, dimensions={0}, use_global_device_ids=true | all-gather | bytes 66560 | tf_op jit(solution)/shard_map/all_gather | solution.py:21
  442.6 4.9 while.25
  447.6 0.2 fusion.29
  447.8 5.5 convolution_bitcast_fusion
  453.3 272.6 %all-reduce.3 = (bf16[4096,2,128]{0,2,1:T(8,128)(2,1)S(1)}, f32[2,128]{1,0:T(2,128)S(1)}) all-reduce(f32[4096,2,128]{0,2,1:T(8,128)} %convolution_bitcast_fusion, f32[2,128]{1,0:T(2,128)S(1)} %get-tuple-element.373), channel_id=1, replica_groups=mesh['vocab'=64,'tok'=8] {'vocab'}, use_global_device_ids=true, to_apply=%region_10.11 | all-reduce | flops 1048832 | bytes 6293504 | tf_op jit(solution)/shard_map/psum | solution.py:130
  726.0 145.3 %collective-permute-start.1 = (bf16[2,1,64]{2,1,0:T(2,128)(2,1)S(1)}, bf16[2,1,64]{2,1,0:T(2,128)(2,1)S(1)}, u32[]{:S(2)}, u32[]{:S(2)}) collective-permute-start(bf16[2,1,64]{2,1,0:T(2,128)(2,1)S(1)} %slice.64), channel_id=1, source_target_pairs={{1,0},{2,1},{3,2},{4,3},{5,4},{6,5},{7,6},{9,8},{10,9},{11,10},{12... | collective-permute-start | bytes 776 | tf_op jit(solution)/shard_map/ppermute | solution.py:17
  871.3 0.6 constant_dynamic-slice_fusion.6
  872.0 2.1 collective-permute-done.1
  874.1 0.7 copy.53
  (172 shorter events, 5.2 us)
Async XLA Ops:
  7.2 33.1 %copy-start = (bf16[128,2048]{1,0:T(8,128)(2,1)S(1)}, bf16[128,2048]{1,0:T(8,128)(2,1)}, u32[]{:S(2)}) copy-start(bf16[128,2048]{1,0:T(8,128)(2,1)} %param.6) | copy-start | bytes 1572868
  7.2 307.9 %all-gather.12.cloned.1.call-start = ((), (), s32[]{:S(2)}) async-start(), calls=%async_computation.2 | async-start | bytes 2129920 | tf_op jit(solution)/shard_map/all_gather | solution.py:95
  8.1 8.9 %collective-permute-start = (bf16[2,1,64]{1,2,0:T(8,128)(2,1)S(1)}, bf16[2,1,64]{1,2,0:T(8,128)(2,1)S(1)}, u32[]{:S(2)}, u32[]{:S(2)}) collective-permute-start(bf16[2,1,64]{1,2,0:T(8,128)(2,1)S(1)} %slice.34), channel_id=1, source_target_pairs={{0,1},{1,2},{2,3},{3,4},{4,5},{5,6},{6,7},{8,9},{9,10},{10,11},{11... | collective-permute-start | bytes 776 | tf_op jit(solution)/shard_map/ppermute | solution.py:17
  23.8 152.8 %all-to-all-start = ((bf16[64,2,1024]{2,1,0:T(2,128)(2,1)}), bf16[64,2,1024]{2,1,0:T(2,128)(2,1)S(1)}, u32[]{:S(2)}, u32[]{:S(2)}) async-start(bf16[64,2,1024]{2,1,0:T(2,128)(2,1)} %reshape.246), calls=%async_computation | async-start | bytes 524288 | tf_op jit(solution)/shard_map/all_to_all | solution.py:67
  180.3 23.6 %all-to-all-start.1 = ((bf16[2,64,512]{2,0,1:T(2,128)(2,1)}), bf16[2,64,512]{2,0,1:T(2,128)(2,1)S(1)}, u32[]{:S(2)}, u32[]{:S(2)}) async-start(bf16[2,64,512]{2,0,1:T(2,128)(2,1)} %copy.46), calls=%async_computation.1 | async-start | bytes 262144 | tf_op jit(solution)/shard_map/all_to_all | solution.py:101
  726.0 148.1 %collective-permute-start.1 = (bf16[2,1,64]{2,1,0:T(2,128)(2,1)S(1)}, bf16[2,1,64]{2,1,0:T(2,128)(2,1)S(1)}, u32[]{:S(2)}, u32[]{:S(2)}) collective-permute-start(bf16[2,1,64]{2,1,0:T(2,128)(2,1)S(1)} %slice.64), channel_id=1, source_target_pairs={{1,0},{2,1},{3,2},{4,3},{5,4},{6,5},{7,6},{9,8},{10,9},{11,10},{12... | collective-permute-start | bytes 776 | tf_op jit(solution)/shard_map/ppermute | solution.py:17
Sparse Core Ops, SparseCore 0:
  17.8 134.5 all-gather.11
where the time goes:
time: 882 us
  blocking collectives  640 us (73%)
  starting transfers between devices  175 us (20%)
  waiting for transfers between devices  19.2 us (2%)
  between operations  15 us (2%)
  local copies, waits for them, and re-layouts  11.9 us (1%)
  other arithmetic  10.5 us (1%)
  matrix products  9.62 us (1%)
    all_gather x6, blocking collectives, joined(): gathered = jax.tree.map(lambda a: lax.all_gather(a, axis), part)  367 us
    psum x1, blocking collectives, on_device(): lax.psum(jnp.einsum('cd,stc->dst', columns, returned, preferred_element_t...  273 us
    ppermute x2, starting transfers between devices, from_behind(): return lax.ppermute(value, axis, pairs)  150 us
  transfers between devices with their start and end apart: 5, of which 3 were waited for; matrix products, arithmetic and copies ran while one was open for 2% of the time, Pallas kernels for 0%

commit v1 on v0

v1 whole, which is shorter than its diff:
```python
import jax
import jax.numpy as jnp
from jax import lax
from jax.experimental import pallas as pl
from jax.experimental.pallas import tpu as pltpu
from jax.sharding import PartitionSpec as P

BF = jnp.bfloat16
F32 = jnp.float32
I32 = jnp.int32
MESH = pl.DeviceIdType.MESH
XT_DTYPE = F32

AG1, A2A1, TST, AG2, AGX, A2A2, NBR, STX, STZ, LOS, RSX, RSN, RSS, HEAD = (
    0, 3, 4, 5, 9, 21, 22, 23, 26, 41, 42, 54, 58, 61)
N_SEMS = 62


def nt(a, b):
    return lax.dot_general(a, b, (((1,), (1,)), ((), ())), preferred_element_type=F32)


def mm(a, b):
    return lax.dot_general(a, b, (((1,), (0,)), ((), ())), preferred_element_type=F32)


def onehot(mask):
    return jnp.where(mask, 1.0, 0.0).astype(BF)


def combine(packs):
    t_max = packs[0][0:2]
    k_max = packs[0][4:6]
    d_max = packs[0][8:10]
    for p in packs[1:]:
        t_max = jnp.maximum(t_max, p[0:2])
        k_max = jnp.maximum(k_max, p[4:6])
        d_max = jnp.maximum(d_max, p[8:10])
    t_sum = jnp.zeros((2, 128), F32)
    k_sum = jnp.zeros((2, 128), F32)
    d_sum = jnp.zeros((2, 128), F32)
    term = jnp.zeros((2, 128), F32)
    for p in packs:
        scale = jnp.exp(p[4:6] - k_max)
        t_sum += p[2:4] * jnp.exp(p[0:2] - t_max)
        k_sum += p[6:8] * scale
        d_sum += p[10:12] * jnp.exp(p[8:10] - d_max)
        term += scale * (p[12:14] + p[6:8] * (d_max - p[8:10]))
    return t_max, t_sum, k_max, k_sum, d_max, d_sum, term


def kernel(tl, hid, head_hbm, bmap, grad_out, loss_out,
           head, head_t, xt, send1, recv1, send2, recv2, pick_sel, place, logits,
           tst_send, tst_recv, nbr_send, nbr_recv, stx_send, stx_recv, stz_send, stz_recv,
           los_send, los_recv, wide, own, rsx_send, rsx_recv, rsn_send, rsn_recv, rss_send, rss_recv,
           s_sem, r_sem):
    v = lax.axis_index("vocab")
    t = lax.axis_index("tok")
    z = v // 4
    x = lax.rem(v, 4)
    a = z // 4
    b = lax.rem(z, 4)

    def at_z(off):
        return (lax.rem(z + off + 16, 16) * 4 + x, t)

    def at_x(off):
        return (z * 4 + lax.rem(x + off, 4), t)

    before = (v, lax.rem(t + 7, 8))
    after = (v, lax.rem(t + 1, 8))

    def copy(k, src, dst, dev):
        return pltpu.make_async_remote_copy(
            src_ref=src, dst_ref=dst, send_sem=s_sem.at[k], recv_sem=r_sem.at[k],
            device_id=dev, device_id_type=MESH)

    sent = []

    def send(k, src, dst, dev):
        c = copy(k, src, dst, dev)
        c.start()
        sent.append(c)
        return c

    head_copy = pltpu.make_async_copy(head_hbm, head, r_sem.at[HEAD])
    head_copy.start()

    barrier = pltpu.get_barrier_semaphore()

    def greet(i, c):
        pl.semaphore_signal(barrier, 1, device_id=(lax.rem(v + i, 64), t), device_id_type=MESH)
        return c

    lax.fori_loop(1, 64, greet, 0)
    pl.semaphore_signal(barrier, 1, device_id=before, device_id_type=MESH)
    pl.semaphore_signal(barrier, 1, device_id=after, device_id_type=MESH)

    eye64 = onehot(lax.broadcasted_iota(I32, (64, 64), 0) == lax.broadcasted_iota(I32, (64, 64), 1))
    for s in range(2):
        xt[a, b, x, :, s * 128:(s + 1) * 128] = nt(eye64, hid[s]).astype(BF)

    bm_row = bmap[...]
    own_row = bm_row // 16
    loc_row = (bm_row - own_row * 16).astype(F32)
    own_row = own_row.astype(F32)
    sub = lax.broadcasted_iota(I32, (256, 256), 0)
    lane = lax.broadcasted_iota(I32, (256, 256), 1)
    own_all = jnp.broadcast_to(own_row, (256, 256))
    own_col = jnp.sum(jnp.where(sub == lane, own_all, 0.0), axis=1, keepdims=True)
    rank_row = jnp.sum(jnp.where((own_col == own_all) & (sub < lane), 1.0, 0.0), axis=0, keepdims=True)
    place_row = own_row * 16.0 + rank_row * 2.0
    row16 = lax.broadcasted_iota(I32, (16, 256), 0)
    mine = (jnp.broadcast_to(own_row, (16, 256)) == v.astype(F32)) & (
        jnp.broadcast_to(rank_row, (16, 256)) == (row16 // 2).astype(F32))
    found = jnp.sum(jnp.where(mine, 1.0, 0.0), axis=1, keepdims=True)
    block = jnp.sum(jnp.where(mine, jnp.broadcast_to(loc_row, (16, 256)), 0.0), axis=1, keepdims=True)
    odd = lax.rem(lax.broadcasted_iota(I32, (16, 1), 0), 2)
    first = jnp.where(found > 0.0, block.astype(I32) * 128 + odd, -4096)
    away = lax.broadcasted_iota(I32, (16, 2048), 1) - first

    pl.semaphore_wait(barrier, 65)

    for j in range(1, 4):
        mine_xt = xt.at[a, b, x]
        send(AG1 + j - 1, mine_xt, mine_xt, at_z(4 * j))

    def pick1(g, c):
        sel = jnp.concatenate([onehot(away == 2 * (8 * g + k)) for k in range(8)], axis=0)
        send1[pl.ds(8 * g, 8)] = nt(sel, tl[...]).astype(BF).reshape(8, 16, 128)
        return c

    lax.fori_loop(0, 8, pick1, 0)

    def spread1(i, c):
        p = lax.rem(v + i, 64)
        copy(A2A1, send1.at[p], recv1.at[v], (p, t)).start()
        return c

    lax.fori_loop(1, 64, spread1, 0)
    pltpu.make_async_copy(send1.at[v], recv1.at[v], r_sem.at[A2A1]).start()

    top = tl[:, 0:128].astype(F32)
    for k in range(1, 16):
        top = jnp.maximum(top, tl[:, k * 128:(k + 1) * 128].astype(F32))
    top_col = jnp.max(top, axis=1, keepdims=True)
    total = jnp.zeros((128, 128), F32)
    for k in range(16):
        total += jnp.exp(tl[:, k * 128:(k + 1) * 128].astype(F32) - top_col)
    t_max = jnp.max(top.T, axis=0, keepdims=True)
    t_sum = jnp.sum(total.T, axis=0, keepdims=True)
    tst_send[...] = jnp.concatenate([t_max, t_sum, jnp.zeros((6, 128), F32)], axis=0)
    tst = send(TST, tst_send, tst_recv, before)

    def along_x(o):
        bb = lax.rem(b + o, 4)
        for j in range(1, 4):
            ref = xt.at[:, bb, x]
            send(AGX + 3 * o + j - 1, ref, ref, at_x(j))

    ag1 = [copy(AG1 + j - 1, xt.at[lax.rem(a + 4 - j, 4), b, x], xt.at[lax.rem(a + 4 - j, 4), b, x], at_z(4))
           for j in range(1, 4)]
    for c in ag1:
        c.wait_recv()
    send(AG2, xt.at[:, b, x], xt.at[:, b, x], at_z(1))
    send(AG2 + 1, xt.at[:, b, x], xt.at[:, b, x], at_z(-1))
    send(AG2 + 2, xt.at[pl.ds(0, 2), b, x], xt.at[pl.ds(0, 2), b, x], at_z(-2))
    send(AG2 + 3, xt.at[pl.ds(2, 2), b, x], xt.at[pl.ds(2, 2), b, x], at_z(2))
    along_x(0)

    r512 = lax.broadcasted_iota(I32, (512, 256), 0) // 2
    l512 = lax.broadcasted_iota(I32, (512, 256), 1)
    source = jnp.sum(jnp.where(r512 == l512, jnp.broadcast_to(place_row, (512, 256)), 0.0), axis=1, keepdims=True)
    source = source.astype(I32) + lax.rem(lax.broadcasted_iota(I32, (512, 1), 0), 2)
    pick_sel[...] = onehot(lax.broadcasted_iota(I32, (512, 1024), 1) == source)
    rr = lax.broadcasted_iota(I32, (512, 1), 0)
    goes = (lax.rem(rr, 128) // 2) * 8 + (rr // 128) * 2 + lax.rem(rr, 2)
    place[...] = onehot(lax.broadcasted_iota(I32, (512, 512), 1) == goes)

    def got_x(ref_of, k, dev):
        copy(k, ref_of, ref_of, dev).wait_recv()

    b_prev = lax.rem(b + 3, 4)
    b_next = lax.rem(b + 1, 4)
    b_far = lax.rem(b + 2, 4)
    got_x(xt.at[:, b_prev, x], AG2, at_z(1))
    along_x(3)
    got_x(xt.at[:, b_next, x], AG2 + 1, at_z(1))
    along_x(1)
    got_x(xt.at[pl.ds(0, 2), b_far, x], AG2 + 2, at_z(1))
    got_x(xt.at[pl.ds(2, 2), b_far, x], AG2 + 3, at_z(1))
    along_x(2)

    pltpu.make_async_copy(recv1, recv1, r_sem.at[A2A1]).wait()
    send2[...] = mm(pick_sel[...], recv1[...].reshape(1024, 128)).reshape(64, 8, 128).astype(BF)

    def spread2(i, c):
        p = lax.rem(v + i, 64)
        copy(A2A2, send2.at[p], recv2.at[v], (p, t)).start()
        return c

    lax.fori_loop(1, 64, spread2, 0)
    pltpu.make_async_copy(send2.at[v], recv2.at[v], r_sem.at[A2A2]).start()

    head_copy.wait()
    eye256 = onehot(sub == lane)

    def turn(i, c):
        cols = pl.ds(pl.multiple_of(i * 256, 256), 256)
        head_t[cols, :] = nt(eye256, head[:, cols]).astype(BF)
        return c

    lax.fori_loop(0, 16, turn, 0)

    logits[...] = jnp.zeros((512, 256), F32)
    for o in (0, 3, 1, 2):
        bb = lax.rem(b + o, 4)
        for j in range(1, 4):
            ref = xt.at[:, bb, lax.rem(x + 4 - j, 4)]
            got_x(ref, AGX + 3 * o + j - 1, at_x(1))

        def forward(i, c):
            cols = pl.ds(pl.multiple_of((i * 4 + bb) * 256, 256), 256)
            logits[...] += mm(head[:, cols], xt[i, bb].reshape(256, 256))
            return c

        lax.fori_loop(0, 4, forward, 0)

    pltpu.make_async_copy(recv2, recv2, r_sem.at[A2A2]).wait()
    picked = mm(place[...], recv2[...].reshape(512, 128)).astype(BF)
    r8 = lax.broadcasted_iota(I32, (8, 128), 0)
    l8 = lax.broadcasted_iota(I32, (8, 128), 1)
    nbr_send[...] = nt(onehot((r8 == 0) & (l8 == 0)), picked)
    nbr = send(NBR, nbr_send, nbr_recv, before)
    low = logits[...].astype(BF).astype(F32)
    d_max = jnp.max(low, axis=0, keepdims=True)
    d_sum = jnp.sum(jnp.exp(low - d_max), axis=0, keepdims=True)
    sub128 = lax.broadcasted_iota(I32, (128, 128), 0)
    lane128 = lax.broadcasted_iota(I32, (128, 128), 1)
    nbr.wait_recv()
    moved = mm(picked, onehot(sub128 == lane128 + 1)) + lax.dot_general(
        nbr_recv[...].astype(BF), onehot((r8 == 0) & (l8 == 127)),
        (((0,), (0,)), ((), ())), preferred_element_type=F32)
    picked2 = jnp.concatenate([picked.astype(F32), moved], axis=1)
    k_max = jnp.max(picked2, axis=0, keepdims=True)
    rel = jnp.exp(picked2 - k_max)
    k_sum = jnp.sum(rel, axis=0, keepdims=True)
    term = jnp.sum(rel * (d_max - low), axis=0, keepdims=True)
    tst.wait_recv()
    l1 = lax.broadcasted_iota(I32, (1, 128), 1)

    def moved_row(row, other):
        return jnp.where(l1 == 127, pltpu.roll(other, 127, 1), pltpu.roll(row, 127, 1))

    halves = lambda r: [r[:, 0:128], r[:, 128:256]]
    rows = [t_max, moved_row(t_max, tst_recv[0:1, :]), t_sum, moved_row(t_sum, tst_recv[1:2, :])]
    for r in (k_max, k_sum, d_max, d_sum, term):
        rows += halves(r)
    rows.append(jnp.zeros((2, 128), F32))
    stx_send[...] = jnp.concatenate(rows, axis=0)
    stx = [send(STX + j - 1, stx_send, stx_recv.at[j - 1], at_x(j)) for j in range(1, 4)]
    for c in stx:
        c.wait_recv()
    merged = combine([stx_send[...]] + [stx_recv[j] for j in range(3)])
    stz_send[...] = jnp.concatenate(list(merged) + [jnp.zeros((2, 128), F32)], axis=0)
    stz = [send(STZ + j - 1, stz_send, stz_recv.at[j - 1], at_z(j)) for j in range(1, 16)]
    for c in stz:
        c.wait_recv()
    t_max, t_sum, k_max, k_sum, d_max, d_sum, term = combine(
        [stz_send[...]] + [stz_recv[j] for j in range(15)])
    t_lse = t_max + jnp.log(t_sum)
    lift = jnp.log(d_sum)
    d_lse = d_max + lift
    scale = jnp.exp(k_max - t_lse)
    mass = k_sum * scale
    loss = scale * (term + k_sum * lift)
    los_send[...] = jnp.concatenate([loss, jnp.zeros((6, 128), F32)], axis=0)
    los = send(LOS, los_send, los_recv, after)

    wide_row = lambda r: jnp.concatenate([r[0:1], r[1:2]], axis=1)
    l256 = lax.broadcasted_iota(I32, (1, 256), 1)
    keep = jnp.where((l256 == 255) & (t == 7), 0.0, 64.0)
    low = logits[...].astype(BF).astype(F32)
    grads = (keep * (wide_row(mass) * jnp.exp(low - wide_row(d_lse))
                     - jnp.exp(picked2 - wide_row(t_lse)))).astype(BF)

    for o in (1, 3, 2, 0):
        bb = lax.rem(b + o, 4)

        def backward(i, c):
            cols = pl.ds(pl.multiple_of((i * 4 + bb) * 256, 256), 256)
            part = mm(head_t[cols, :], grads).reshape(4, 64, 256)
            wide[...] = part
            own[o, i] = wide[x]
            for k in range(4):
                rsx_send[o, k, i] = part[k].astype(XT_DTYPE)
            return c

        lax.fori_loop(0, 4, backward, 0)
        for j in range(1, 4):
            send(RSX + 3 * o + j - 1, rsx_send.at[o, lax.rem(x + j, 4)], rsx_recv.at[o, j - 1], at_x(j))

    def summed(o, into):
        for j in range(1, 4):
            ref = rsx_recv.at[o, j - 1]
            copy(RSX + 3 * o + j - 1, ref, ref, at_x(1)).wait_recv()

        def add(i, c):
            into[i] = own[o, i] + rsx_recv[o, 0, i].astype(F32) + rsx_recv[o, 1, i].astype(F32) + rsx_recv[o, 2, i].astype(F32)
            return c

        lax.fori_loop(0, 4, add, 0)

    summed(1, rsn_send.at[0])
    n0 = send(RSN, rsn_send.at[0], rsn_recv.at[0], at_z(1))
    summed(3, rsn_send.at[1])
    n1 = send(RSN + 1, rsn_send.at[1], rsn_recv.at[1], at_z(-1))
    summed(2, rsn_send.at[2])
    n2 = send(RSN + 2, rsn_send.at[2, pl.ds(0, 2)], rsn_recv.at[2, pl.ds(0, 2)], at_z(-2))
    n3 = send(RSN + 3, rsn_send.at[2, pl.ds(2, 2)], rsn_recv.at[2, pl.ds(2, 2)], at_z(2))
    summed(0, rss_send)

    los.wait_recv()
    here = los_send[...]
    other = los_recv[...]
    l8b = lax.broadcasted_iota(I32, (8, 128), 1)
    late = jnp.where(l8b == 0, jnp.where(t == 0, 0.0, pltpu.roll(other, 1, 1)), pltpu.roll(here, 1, 1))
    both = jnp.concatenate([here[0:1], late[1:2]], axis=0)
    l2 = lax.broadcasted_iota(I32, (2, 128), 1)
    for k in range(2):
        loss_out[:, k:k + 1] = jnp.sum(jnp.where(l2 == 2 * v + k, both, 0.0), axis=1, keepdims=True)

    for c in (n0, n1, n2, n3):
        c.wait_recv()

    def add_near(i, c):
        rss_send[i] = rss_send[i] + rsn_recv[0, i] + rsn_recv[1, i] + rsn_recv[2, i]
        return c

    lax.fori_loop(0, 4, add_near, 0)
    far = [send(RSS + j - 1, rss_send.at[lax.rem(a + j, 4)], rss_recv.at[j - 1], at_z(4 * j)) for j in range(1, 4)]
    for c in far:
        c.wait_recv()
    grad = (rss_send[a] + rss_recv[0] + rss_recv[1] + rss_recv[2]).astype(BF)
    eye128 = onehot(sub128 == lane128)
    for s in range(2):
        grad_out[s] = nt(eye128, grad[:, s * 128:(s + 1) * 128]).astype(BF)

    for c in sent:
        c.wait_send()
    for k, ref in ((A2A1, send1), (A2A2, send2)):
        most = ref.at[pl.ds(0, 63)]
        pltpu.make_async_copy(most, most, s_sem.at[k]).wait()


def on_device(target_logits, draft_hidden, draft_head, block_map):
    vm = pl.BlockSpec(memory_space=pltpu.VMEM)
    v = pltpu.VMEM
    return pl.pallas_call(
        kernel,
        name="draft_loss",
        out_shape=(jax.ShapeDtypeStruct((2, 128, 64), BF), jax.ShapeDtypeStruct((2, 2), F32)),
        in_specs=[vm, vm, pl.BlockSpec(memory_space=pl.ANY), vm],
        out_specs=(vm, vm),
        scratch_shapes=[
            v((512, 4096), BF), v((4096, 512), BF), v((4, 4, 4, 64, 256), BF),
            v((64, 16, 128), BF), v((64, 16, 128), BF), v((64, 8, 128), BF), v((64, 8, 128), BF),
            v((512, 1024), BF), v((512, 512), BF), v((512, 256), F32),
            v((8, 128), F32), v((8, 128), F32), v((8, 512), F32), v((8, 512), F32),
            v((16, 128), F32), v((3, 16, 128), F32), v((16, 128), F32), v((15, 16, 128), F32),
            v((8, 128), F32), v((8, 128), F32),
            v((4, 64, 256), F32), v((4, 4, 64, 256), F32),
            v((4, 4, 4, 64, 256), XT_DTYPE), v((4, 3, 4, 64, 256), XT_DTYPE),
            v((3, 4, 64, 256), F32), v((3, 4, 64, 256), F32),
            v((4, 64, 256), F32), v((3, 64, 256), F32),
            pltpu.SemaphoreType.DMA((N_SEMS,)), pltpu.SemaphoreType.DMA((N_SEMS,)),
        ],
        compiler_params=pltpu.CompilerParams(
            collective_id=0, has_side_effects=True, vmem_limit_bytes=50 * 1024 * 1024),
        cost_estimate=pl.CostEstimate(flops=2 ** 31, bytes_accessed=5 * 2 ** 20, transcendentals=2 ** 20),
    )(target_logits, draft_hidden, draft_head, block_map.reshape(1, 256))


def solution(mesh):
    return jax.shard_map(
        on_device,
        mesh=mesh,
        in_specs=(P("tok", "vocab"), P(None, "tok", "vocab"), P("vocab", None), P()),
        out_specs=(P(None, "tok", "vocab"), P(None, ("tok", "vocab"))),
        check_vma=False,
    )
```

time: 882 us -> 149 us (0.17)
  blocking collectives: 640 us -> 0 us
  starting transfers between devices: 175 us -> 0 us
  Pallas kernels: 0 us -> 145 us
  waiting for transfers between devices: 19.2 us -> 0 us
  between operations: 15 us -> 0.65 us
  other arithmetic: 10.5 us -> 0 us
  matrix products: 9.62 us -> 0 us
    all_gather x6 -> x0, blocking collectives: 367 us -> none  [joined(): gathered = jax.tree.map(lambda a: lax.all_gather(a, axis), part)]
    psum x1 -> x0, blocking collectives: 273 us -> none  [on_device(): lax.psum(jnp.einsum('cd,stc->dst', columns, returned, preferred_element_t...]
    ppermute x2 -> x0, starting transfers between devices: 150 us -> none  [from_behind(): return lax.ppermute(value, axis, pairs)]
    pallas_call x0 -> x1, Pallas kernels: none -> 145 us  [on_device(): pl.pallas_call(kernel, name='draft_loss', out_shape=(jax.ShapeDtypeStruct...]
    all_to_all x2 -> x0, starting transfers between devices: 24.7 us -> none  [the longest x1 16.2 us: on_device(): lax.all_to_all(compact.reshape(tok_rows, 1, SEL_MAX * BLK), 'vocab', spli...]
    all_to_all x2 -> x0, waiting for transfers between devices: 15 us -> none  [the longest x1 15 us: on_device(): lax.all_to_all(picked.reshape(share, vocab_count, draft_cols), 'vocab', s...]
    dot_general x2 -> x0, matrix products: 9.62 us -> none  [the longest x1 5.5 us: on_device(): jnp.einsum('cd,stc->dst', columns, returned, preferred_element_type=jnp.f...]
  transfers between devices with their start and end apart: 5 -> 0, of which waited for: 3 -> 0; matrix products, arithmetic and copies ran while one was open for 2% -> 0% of each run, Pallas kernels for 0% -> 0%
where the time goes in v1:
time: 149 us
  Pallas kernels  145 us (97%)
  local copies, waits for them, and re-layouts  3.86 us (3%)
    pallas_call x1, Pallas kernels, on_device(): pl.pallas_call(kernel, name='draft_loss', out_shape=(jax.ShapeDtypeStruct...  145 us
    unnamed x6, local copies, waits for them, and re-layouts  3.15 us

profile of v1, /device:TPU:1, one launch (start us, length us, event | category | flops | bytes accessed | tf_op | source)
XLA Modules:
  0.0 149.1 jit_solution(6431034907704463577)
XLA Ops:
  0.6 0.9 copy.6.hid
  1.5 0.0 copy-start
  1.5 1.0 copy-done
  2.6 0.0 copy-start.1
  2.6 0.7 copy-done.1
  3.2 144.6 %draft_loss.1 = (bf16[2,128,64]{2,1,0:T(8,128)(2,1)S(1)}, f32[2,2]{1,0:T(2,128)S(1)}) custom-call(bf16[128,2048]{1,0:T(8,128)(2,1)S(1)} %copy-done, bf16[2,128,64]{2,1,0:T(8,128)(2,1)S(1)} %copy.6.hid, bf16[512,4096]{1,0:T(8,128)(2,1)} %head_hbm.1, s32[1,256]{1,0:T(1,128)S(1)} %bitcast.1), custom_call_target="tpu_custom_call" | custom-call | flops 2147483648 | bytes 5242880 | tf_op jit(solution)/shard_map/draft_loss/pallas_call | solution.py:359
  147.8 0.7 copy.7
  148.5 0.6 copy.9
Async XLA Ops:
  1.5 1.0 copy-start
  2.6 0.7 copy-start.1

commit v2 on v1

--- a/solution.py
+++ b/solution.py
@@ -9,11 +9,16 @@
 F32 = jnp.float32
 I32 = jnp.int32
 MESH = pl.DeviceIdType.MESH
-XT_DTYPE = F32
-
-AG1, A2A1, TST, AG2, AGX, A2A2, NBR, STX, STZ, LOS, RSX, RSN, RSS, HEAD = (
-    0, 3, 4, 5, 9, 21, 22, 23, 26, 41, 42, 54, 58, 61)
-N_SEMS = 62
+XT_DTYPE = BF
+
+COUNTS = dict(AG1=3, A2A1=1, LSX=3, LSZ=15, LSN=1, AG2=4, AGX=12, A2A2=1, NBR=1, STX=3, STZ=15, LOS=1,
+              RSX=24, RSN=8, RSS=6, HEAD=1, TL=1, HID=2, MAP=1)
+BASE = {}
+N_SEMS = 0
+for _name, _count in COUNTS.items():
+    BASE[_name] = N_SEMS
+    N_SEMS += _count
+AG1, A2A1, LSX, LSZ, LSN, AG2, AGX, A2A2, NBR, STX, STZ, LOS, RSX, RSN, RSS, HEAD, TL, HID, MAP = BASE.values()
 
 
 def nt(a, b):
@@ -28,32 +33,36 @@
     return jnp.where(mask, 1.0, 0.0).astype(BF)
 
 
+def combine_lse(packs):
+    top = packs[0][0:1]
+    for p in packs[1:]:
+        top = jnp.maximum(top, p[0:1])
+    total = jnp.zeros((1, 128), F32)
+    for p in packs:
+        total += p[1:2] * jnp.exp(p[0:1] - top)
+    return jnp.concatenate([top, total, jnp.zeros((6, 128), F32)], axis=0)
+
+
 def combine(packs):
-    t_max = packs[0][0:2]
-    k_max = packs[0][4:6]
-    d_max = packs[0][8:10]
+    top = packs[0][0:2]
     for p in packs[1:]:
-        t_max = jnp.maximum(t_max, p[0:2])
-        k_max = jnp.maximum(k_max, p[4:6])
-        d_max = jnp.maximum(d_max, p[8:10])
-    t_sum = jnp.zeros((2, 128), F32)
-    k_sum = jnp.zeros((2, 128), F32)
-    d_sum = jnp.zeros((2, 128), F32)
+        top = jnp.maximum(top, p[0:2])
+    total = jnp.zeros((2, 128), F32)
+    mass = jnp.zeros((2, 128), F32)
     term = jnp.zeros((2, 128), F32)
     for p in packs:
-        scale = jnp.exp(p[4:6] - k_max)
-        t_sum += p[2:4] * jnp.exp(p[0:2] - t_max)
-        k_sum += p[6:8] * scale
-        d_sum += p[10:12] * jnp.exp(p[8:10] - d_max)
-        term += scale * (p[12:14] + p[6:8] * (d_max - p[8:10]))
-    return t_max, t_sum, k_max, k_sum, d_max, d_sum, term
-
-
-def kernel(tl, hid, head_hbm, bmap, grad_out, loss_out,
-           head, head_t, xt, send1, recv1, send2, recv2, pick_sel, place, logits,
-           tst_send, tst_recv, nbr_send, nbr_recv, stx_send, stx_recv, stz_send, stz_recv,
-           los_send, los_recv, wide, own, rsx_send, rsx_recv, rsn_send, rsn_recv, rss_send, rss_recv,
-           s_sem, r_sem):
+        rise = top - p[0:2]
+        total += p[2:4] * jnp.exp(-rise)
+        mass += p[4:6]
+        term += p[6:8] + p[4:6] * rise
+    return top, total, mass, term
+
+
+def kernel(tl_hbm, hid_hbm, head_hbm, bmap_hbm, grad_out, loss_out,
+           bmap, tl, head, head_t, xt, send1, recv1, send2, recv2, pick_sel, place, logits, probs,
+           lsx_send, lsx_recv, lsz_send, lsz_recv, lse_send, lse_recv, nbr_send, nbr_recv,
+           stx_send, stx_recv, stz_send, stz_recv, los_send, los_recv, wide, own,
+           rsx_send, rsx_recv, rsn_send, rsn_recv, rss_send, rss_recv, s_sem, r_sem):
     v = lax.axis_index("vocab")
     t = lax.axis_index("tok")
     z = v // 4
@@ -83,6 +92,14 @@
         sent.append(c)
         return c
 
+    hid_copies = [pltpu.make_async_copy(hid_hbm.at[s], xt.at[a, b, x, :, pl.ds(s * 128, 128)], r_sem.at[HID + s])
+                  for s in range(2)]
+    for c in hid_copies:
+        c.start()
+    map_copy = pltpu.make_async_copy(bmap_hbm, bmap, r_sem.at[MAP])
+    map_copy.start()
+    tl_copy = pltpu.make_async_copy(tl_hbm, tl, r_sem.at[TL])
+    tl_copy.start()
     head_copy = pltpu.make_async_copy(head_hbm, head, r_sem.at[HEAD])
     head_copy.start()
 
@@ -96,10 +113,7 @@
     pl.semaphore_signal(barrier, 1, device_id=before, device_id_type=MESH)
     pl.semaphore_signal(barrier, 1, device_id=after, device_id_type=MESH)
 
-    eye64 = onehot(lax.broadcasted_iota(I32, (64, 64), 0) == lax.broadcasted_iota(I32, (64, 64), 1))
-    for s in range(2):
-        xt[a, b, x, :, s * 128:(s + 1) * 128] = nt(eye64, hid[s]).astype(BF)
-
+    map_copy.wait()
     bm_row = bmap[...]
     own_row = bm_row // 16
     loc_row = (bm_row - own_row * 16).astype(F32)
@@ -119,11 +133,15 @@
     first = jnp.where(found > 0.0, block.astype(I32) * 128 + odd, -4096)
     away = lax.broadcasted_iota(I32, (16, 2048), 1) - first
 
+    for c in hid_copies:
+        c.wait()
     pl.semaphore_wait(barrier, 65)
 
     for j in range(1, 4):
         mine_xt = xt.at[a, b, x]
         send(AG1 + j - 1, mine_xt, mine_xt, at_z(4 * j))
+
+    tl_copy.wait()
 
     def pick1(g, c):
         sel = jnp.concatenate([onehot(away == 2 * (8 * g + k)) for k in range(8)], axis=0)
@@ -149,8 +167,8 @@
         total += jnp.exp(tl[:, k * 128:(k + 1) * 128].astype(F32) - top_col)
     t_max = jnp.max(top.T, axis=0, keepdims=True)
     t_sum = jnp.sum(total.T, axis=0, keepdims=True)
-    tst_send[...] = jnp.concatenate([t_max, t_sum, jnp.zeros((6, 128), F32)], axis=0)
-    tst = send(TST, tst_send, tst_recv, before)
+    lsx_send[...] = jnp.concatenate([t_max, t_sum, jnp.zeros((6, 128), F32)], axis=0)
+    lsx = [send(LSX + j - 1, lsx_send, lsx_recv.at[j - 1], at_x(j)) for j in range(1, 4)]
 
     def along_x(o):
         bb = lax.rem(b + o, 4)
@@ -167,6 +185,11 @@
     send(AG2 + 2, xt.at[pl.ds(0, 2), b, x], xt.at[pl.ds(0, 2), b, x], at_z(-2))
     send(AG2 + 3, xt.at[pl.ds(2, 2), b, x], xt.at[pl.ds(2, 2), b, x], at_z(2))
     along_x(0)
+
+    for c in lsx:
+        c.wait_recv()
+    lsz_send[...] = combine_lse([lsx_send[...]] + [lsx_recv[j] for j in range(3)])
+    lsz = [send(LSZ + j - 1, lsz_send, lsz_recv.at[j - 1], at_z(j)) for j in range(1, 16)]
 
     r512 = lax.broadcasted_iota(I32, (512, 256), 0) // 2
     l512 = lax.broadcasted_iota(I32, (512, 256), 1)
@@ -225,6 +248,12 @@
             return c
 
         lax.fori_loop(0, 4, forward, 0)
+
+    for c in lsz:
+        c.wait_recv()
+    stat = combine_lse([lsz_send[...]] + [lsz_recv[j] for j in range(15)])
+    lse_send[...] = jnp.broadcast_to(stat[0:1] + jnp.log(stat[1:2]), (8, 128))
+    lse_copy = send(LSN, lse_send, lse_recv, before)
 
     pltpu.make_async_copy(recv2, recv2, r_sem.at[A2A2]).wait()
     picked = mm(place[...], recv2[...].reshape(512, 128)).astype(BF)
@@ -242,38 +271,28 @@
         nbr_recv[...].astype(BF), onehot((r8 == 0) & (l8 == 127)),
         (((0,), (0,)), ((), ())), preferred_element_type=F32)
     picked2 = jnp.concatenate([picked.astype(F32), moved], axis=1)
-    k_max = jnp.max(picked2, axis=0, keepdims=True)
-    rel = jnp.exp(picked2 - k_max)
-    k_sum = jnp.sum(rel, axis=0, keepdims=True)
-    term = jnp.sum(rel * (d_max - low), axis=0, keepdims=True)
-    tst.wait_recv()
+    lse_copy.wait_recv()
     l1 = lax.broadcasted_iota(I32, (1, 128), 1)
-
-    def moved_row(row, other):
-        return jnp.where(l1 == 127, pltpu.roll(other, 127, 1), pltpu.roll(row, 127, 1))
-
-    halves = lambda r: [r[:, 0:128], r[:, 128:256]]
-    rows = [t_max, moved_row(t_max, tst_recv[0:1, :]), t_sum, moved_row(t_sum, tst_recv[1:2, :])]
-    for r in (k_max, k_sum, d_max, d_sum, term):
-        rows += halves(r)
-    rows.append(jnp.zeros((2, 128), F32))
+    t_lse = lse_send[0:1, :]
+    moved_lse = jnp.where(l1 == 127, pltpu.roll(lse_recv[0:1, :], 127, 1), pltpu.roll(t_lse, 127, 1))
+    probs[...] = jnp.exp(picked2 - jnp.concatenate([t_lse, moved_lse], axis=1))
+    mass = jnp.sum(probs[...], axis=0, keepdims=True)
+    term = jnp.sum(probs[...] * (d_max - low), axis=0, keepdims=True)
+    rows = []
+    for r in (d_max, d_sum, mass, term):
+        rows += [r[:, 0:128], r[:, 128:256]]
     stx_send[...] = jnp.concatenate(rows, axis=0)
     stx = [send(STX + j - 1, stx_send, stx_recv.at[j - 1], at_x(j)) for j in range(1, 4)]
     for c in stx:
         c.wait_recv()
-    merged = combine([stx_send[...]] + [stx_recv[j] for j in range(3)])
-    stz_send[...] = jnp.concatenate(list(merged) + [jnp.zeros((2, 128), F32)], axis=0)
+    stz_send[...] = jnp.concatenate(combine([stx_send[...]] + [stx_recv[j] for j in range(3)]), axis=0)
     stz = [send(STZ + j - 1, stz_send, stz_recv.at[j - 1], at_z(j)) for j in range(1, 16)]
     for c in stz:
         c.wait_recv()
-    t_max, t_sum, k_max, k_sum, d_max, d_sum, term = combine(
-        [stz_send[...]] + [stz_recv[j] for j in range(15)])
-    t_lse = t_max + jnp.log(t_sum)
+    d_max, d_sum, mass, term = combine([stz_send[...]] + [stz_recv[j] for j in range(15)])
     lift = jnp.log(d_sum)
     d_lse = d_max + lift
-    scale = jnp.exp(k_max - t_lse)
-    mass = k_sum * scale
-    loss = scale * (term + k_sum * lift)
+    loss = term + mass * lift
     los_send[...] = jnp.concatenate([loss, jnp.zeros((6, 128), F32)], axis=0)
     los = send(LOS, los_send, los_recv, after)
 
@@ -282,7 +301,11 @@
     keep = jnp.where((l256 == 255) & (t == 7), 0.0, 64.0)
     low = logits[...].astype(BF).astype(F32)
     grads = (keep * (wide_row(mass) * jnp.exp(low - wide_row(d_lse))
-                     - jnp.exp(picked2 - wide_row(t_lse)))).astype(BF)
+                     - probs[...])).astype(BF)
+
+    def along_x_back(s, o):
+        for j in range(1, 4):
+            send(RSX + 12 * s + 3 * o + j - 1, rsx_send.at[s, o, lax.rem(x + j, 4)], rsx_recv.at[s, o, j - 1], at_x(j))
 
     for o in (1, 3, 2, 0):
         bb = lax.rem(b + o, 4)
@@ -291,34 +314,66 @@
             cols = pl.ds(pl.multiple_of((i * 4 + bb) * 256, 256), 256)
             part = mm(head_t[cols, :], grads).reshape(4, 64, 256)
             wide[...] = part
-            own[o, i] = wide[x]
-            for k in range(4):
-                rsx_send[o, k, i] = part[k].astype(XT_DTYPE)
+            for s in range(2):
+                half = slice(s * 128, (s + 1) * 128)
+                own[s, o, i] = wide[x, :, half]
+                for k in range(4):
+                    rsx_send[s, o, k, i] = part[k, :, half].astype(XT_DTYPE)
             return c
 
         lax.fori_loop(0, 4, backward, 0)
+        along_x_back(0, o)
+    for o in (1, 3, 2, 0):
+        along_x_back(1, o)
+
+    def summed(s, o, into):
         for j in range(1, 4):
-            send(RSX + 3 * o + j - 1, rsx_send.at[o, lax.rem(x + j, 4)], rsx_recv.at[o, j - 1], at_x(j))
-
-    def summed(o, into):
-        for j in range(1, 4):
-            ref = rsx_recv.at[o, j - 1]
-            copy(RSX + 3 * o + j - 1, ref, ref, at_x(1)).wait_recv()
+            ref = rsx_recv.at[s, o, j - 1]
+            copy(RSX + 12 * s + 3 * o + j - 1, ref, ref, at_x(1)).wait_recv()
 
         def add(i, c):
-            into[i] = own[o, i] + rsx_recv[o, 0, i].astype(F32) + rsx_recv[o, 1, i].astype(F32) + rsx_recv[o, 2, i].astype(F32)
+            into[i] = own[s, o, i] + rsx_recv[s, o, 0, i].astype(F32) + rsx_recv[s, o, 1, i].astype(F32) + rsx_recv[s, o, 2, i].astype(F32)
             return c
 
         lax.fori_loop(0, 4, add, 0)
 
-    summed(1, rsn_send.at[0])
-    n0 = send(RSN, rsn_send.at[0], rsn_recv.at[0], at_z(1))
-    summed(3, rsn_send.at[1])
-    n1 = send(RSN + 1, rsn_send.at[1], rsn_recv.at[1], at_z(-1))
-    summed(2, rsn_send.at[2])
-    n2 = send(RSN + 2, rsn_send.at[2, pl.ds(0, 2)], rsn_recv.at[2, pl.ds(0, 2)], at_z(-2))
-    n3 = send(RSN + 3, rsn_send.at[2, pl.ds(2, 2)], rsn_recv.at[2, pl.ds(2, 2)], at_z(2))
-    summed(0, rss_send)
+    near = {0: [], 1: []}
+
+    def to_near(s, o):
+        k = RSN + 4 * s
+        if o == 1:
+            summed(s, o, rsn_send.at[s, 0])
+            near[s].append(send(k, rsn_send.at[s, 0], rsn_recv.at[s, 0], at_z(1)))
+        elif o == 3:
+            summed(s, o, rsn_send.at[s, 1])
+            near[s].append(send(k + 1, rsn_send.at[s, 1], rsn_recv.at[s, 1], at_z(-1)))
+        else:
+            summed(s, o, rsn_send.at[s, 2])
+            low2, high2 = pl.ds(0, 2), pl.ds(2, 2)
+            near[s].append(send(k + 2, rsn_send.at[s, 2, low2], rsn_recv.at[s, 2, low2], at_z(-2)))
+            near[s].append(send(k + 3, rsn_send.at[s, 2, high2], rsn_recv.at[s, 2, high2], at_z(2)))
+
+    def to_far(s):
+        for c in near[s]:
+            c.wait_recv()
+
+        def add_near(i, c):
+            rss_send[s, i] = rss_send[s, i] + rsn_recv[s, 0, i] + rsn_recv[s, 1, i] + rsn_recv[s, 2, i]
+            return c
+
+        lax.fori_loop(0, 4, add_near, 0)
+        return [send(RSS + 3 * s + j - 1, rss_send.at[s, lax.rem(a + j, 4)], rss_recv.at[s, j - 1], at_z(4 * j))
+                for j in range(1, 4)]
+
+    for o in (1, 3, 2):
+        to_near(0, o)
+    summed(0, 0, rss_send.at[0])
+    to_near(1, 1)
+    far = to_far(0)
+    to_near(1, 3)
+    to_near(1, 2)
+    summed(1, 0, rss_send.at[1])
+    far += to_far(1)
 
     los.wait_recv()
     here = los_send[...]
@@ -330,21 +385,10 @@
     for k in range(2):
         loss_out[:, k:k + 1] = jnp.sum(jnp.where(l2 == 2 * v + k, both, 0.0), axis=1, keepdims=True)
 
-    for c in (n0, n1, n2, n3):
-        c.wait_recv()
-
-    def add_near(i, c):
-        rss_send[i] = rss_send[i] + rsn_recv[0, i] + rsn_recv[1, i] + rsn_recv[2, i]
-        return c
-
-    lax.fori_loop(0, 4, add_near, 0)
-    far = [send(RSS + j - 1, rss_send.at[lax.rem(a + j, 4)], rss_recv.at[j - 1], at_z(4 * j)) for j in range(1, 4)]
     for c in far:
         c.wait_recv()
-    grad = (rss_send[a] + rss_recv[0] + rss_recv[1] + rss_recv[2]).astype(BF)
-    eye128 = onehot(sub128 == lane128)
     for s in range(2):
-        grad_out[s] = nt(eye128, grad[:, s * 128:(s + 1) * 128]).astype(BF)
+        grad_out[s] = (rss_send[s, a] + rss_recv[s, 0] + rss_recv[s, 1] + rss_recv[s, 2]).astype(BF)
 
     for c in sent:
         c.wait_send()
@@ -355,30 +399,32 @@
 
 def on_device(target_logits, draft_hidden, draft_head, block_map):
     vm = pl.BlockSpec(memory_space=pltpu.VMEM)
+    hbm = pl.BlockSpec(memory_space=pltpu.HBM)
     v = pltpu.VMEM
-    return pl.pallas_call(
+    tile = v((8, 128), F32)
+    grad, loss = pl.pallas_call(
         kernel,
         name="draft_loss",
-        out_shape=(jax.ShapeDtypeStruct((2, 128, 64), BF), jax.ShapeDtypeStruct((2, 2), F32)),
-        in_specs=[vm, vm, pl.BlockSpec(memory_space=pl.ANY), vm],
+        out_shape=(jax.ShapeDtypeStruct((2, 64, 128), BF), jax.ShapeDtypeStruct((2, 2), F32)),
+        in_specs=[hbm, hbm, hbm, hbm],
         out_specs=(vm, vm),
         scratch_shapes=[
-            v((512, 4096), BF), v((4096, 512), BF), v((4, 4, 4, 64, 256), BF),
+            v((1, 256), I32), v((128, 2048), BF), v((512, 4096), BF), v((4096, 512), BF), v((4, 4, 4, 64, 256), BF),
             v((64, 16, 128), BF), v((64, 16, 128), BF), v((64, 8, 128), BF), v((64, 8, 128), BF),
-            v((512, 1024), BF), v((512, 512), BF), v((512, 256), F32),
-            v((8, 128), F32), v((8, 128), F32), v((8, 512), F32), v((8, 512), F32),
-            v((16, 128), F32), v((3, 16, 128), F32), v((16, 128), F32), v((15, 16, 128), F32),
-            v((8, 128), F32), v((8, 128), F32),
-            v((4, 64, 256), F32), v((4, 4, 64, 256), F32),
-            v((4, 4, 4, 64, 256), XT_DTYPE), v((4, 3, 4, 64, 256), XT_DTYPE),
-            v((3, 4, 64, 256), F32), v((3, 4, 64, 256), F32),
-            v((4, 64, 256), F32), v((3, 64, 256), F32),
+            v((512, 1024), BF), v((512, 512), BF), v((512, 256), F32), v((512, 256), F32),
+            tile, v((3, 8, 128), F32), tile, v((15, 8, 128), F32), tile, tile, v((8, 512), F32), v((8, 512), F32),
+            tile, v((3, 8, 128), F32), tile, v((15, 8, 128), F32), tile, tile,
+            v((4, 64, 256), F32), v((2, 4, 4, 64, 128), F32),
+            v((2, 4, 4, 4, 64, 128), XT_DTYPE), v((2, 4, 3, 4, 64, 128), XT_DTYPE),
+            v((2, 3, 4, 64, 128), F32), v((2, 3, 4, 64, 128), F32),
+            v((2, 4, 64, 128), F32), v((2, 3, 64, 128), F32),
             pltpu.SemaphoreType.DMA((N_SEMS,)), pltpu.SemaphoreType.DMA((N_SEMS,)),
         ],
         compiler_params=pltpu.CompilerParams(
-            collective_id=0, has_side_effects=True, vmem_limit_bytes=50 * 1024 * 1024),
+            collective_id=0, has_side_effects=True, vmem_limit_bytes=62 * 1024 * 1024),
         cost_estimate=pl.CostEstimate(flops=2 ** 31, bytes_accessed=5 * 2 ** 20, transcendentals=2 ** 20),
-    )(target_logits, draft_hidden, draft_head, block_map.reshape(1, 256))
+    )(target_logits, draft_hidden.transpose(0, 2, 1), draft_head, block_map.reshape(1, 256))
+    return grad.transpose(0, 2, 1), loss
 
 
 def solution(mesh):

time: 149 us -> 123 us (0.83)
  Pallas kernels: 145 us -> 119 us
    pallas_call x1, Pallas kernels: 145 us -> 119 us  [on_device(): pl.pallas_call(kernel, name='draft_loss', out_shape=(jax.ShapeDtypeStruct...]
    unnamed x6 -> x2, local copies, waits for them, and re-layouts: 3.15 us -> 2.6 us
where the time goes in v2:
time: 123 us; the launch traced here: 122 us
  Pallas kernels  119 us (97%)
  local copies, waits for them, and re-layouts  2.6 us (2%)
    pallas_call x1, Pallas kernels, on_device(): pl.pallas_call(kernel, name='draft_loss', out_shape=(jax.ShapeDtypeStruct...  119 us
    unnamed x2, local copies, waits for them, and re-layouts  2.6 us

profile of v2, /device:TPU:1, one launch (start us, length us, event | category | flops | bytes accessed | tf_op | source)
XLA Modules:
  0.0 122.5 jit_solution(8510250087031438851)
XLA Ops:
  0.6 119.3 %draft_loss.1 = (bf16[2,64,128]{2,1,0:T(8,128)(2,1)}, f32[2,2]{1,0:T(2,128)}) custom-call(bf16[128,2048]{1,0:T(8,128)(2,1)} %tl_hbm.1, bf16[2,64,128]{2,1,0:T(8,128)(2,1)} %bitcast.4, bf16[512,4096]{1,0:T(8,128)(2,1)} %head_hbm.1, s32[1,256]{1,0:T(1,128)} %bitcast.5), custom_call_target="tpu_custom_call" | custom-call | flops 2147483648 | bytes 5242880 | tf_op jit(solution)/shard_map/draft_loss/pallas_call | solution.py:405
  119.9 1.4 %copy.8 = bf16[2,128,64]{1,2,0:T(8,128)(2,1)} copy(bf16[2,128,64]{1,2,0:T(8,128)(2,1)} %bitcast.3) | data formatting | bytes 65536
  121.3 1.2 %copy.9 = f32[2,2]{1,0:T(2,128)} copy(f32[2,2]{1,0:T(2,128)} %get-tuple-element.9) | data formatting | bytes 32

commit v3 on v2

--- a/solution.py
+++ b/solution.py
@@ -11,14 +11,14 @@
 MESH = pl.DeviceIdType.MESH
 XT_DTYPE = BF
 
-COUNTS = dict(AG1=3, A2A1=1, LSX=3, LSZ=15, LSN=1, AG2=4, AGX=12, A2A2=1, NBR=1, STX=3, STZ=15, LOS=1,
+COUNTS = dict(AG1=3, A2A1=1, LSX=3, LSZ=15, LSN=1, AG2=4, AGX=12, A2A2=1, NBR=1, STX=3, STZ=15, LOX=3, LOZ=15, LOS=1,
               RSX=24, RSN=8, RSS=6, HEAD=1, TL=1, HID=2, MAP=1)
 BASE = {}
 N_SEMS = 0
 for _name, _count in COUNTS.items():
     BASE[_name] = N_SEMS
     N_SEMS += _count
-AG1, A2A1, LSX, LSZ, LSN, AG2, AGX, A2A2, NBR, STX, STZ, LOS, RSX, RSN, RSS, HEAD, TL, HID, MAP = BASE.values()
+AG1, A2A1, LSX, LSZ, LSN, AG2, AGX, A2A2, NBR, STX, STZ, LOX, LOZ, LOS, RSX, RSN, RSS, HEAD, TL, HID, MAP = BASE.values()
 
 
 def nt(a, b):
@@ -33,14 +33,14 @@
     return jnp.where(mask, 1.0, 0.0).astype(BF)
 
 
-def combine_lse(packs):
+def combine_target(packs):
     top = packs[0][0:1]
     for p in packs[1:]:
         top = jnp.maximum(top, p[0:1])
-    total = jnp.zeros((1, 128), F32)
+    sums = jnp.zeros((2, 128), F32)
     for p in packs:
-        total += p[1:2] * jnp.exp(p[0:1] - top)
-    return jnp.concatenate([top, total, jnp.zeros((6, 128), F32)], axis=0)
+        sums += p[1:3] * jnp.exp(p[0:1] - top)
+    return jnp.concatenate([top, sums, jnp.zeros((5, 128), F32)], axis=0)
 
 
 def combine(packs):
@@ -48,20 +48,16 @@
     for p in packs[1:]:
         top = jnp.maximum(top, p[0:2])
     total = jnp.zeros((2, 128), F32)
-    mass = jnp.zeros((2, 128), F32)
-    term = jnp.zeros((2, 128), F32)
     for p in packs:
-        rise = top - p[0:2]
-        total += p[2:4] * jnp.exp(-rise)
-        mass += p[4:6]
-        term += p[6:8] + p[4:6] * rise
-    return top, total, mass, term
+        total += p[2:4] * jnp.exp(p[0:2] - top)
+    return jnp.concatenate([top, total], axis=0)
 
 
 def kernel(tl_hbm, hid_hbm, head_hbm, bmap_hbm, grad_out, loss_out,
            bmap, tl, head, head_t, xt, send1, recv1, send2, recv2, pick_sel, place, logits, probs,
            lsx_send, lsx_recv, lsz_send, lsz_recv, lse_send, lse_recv, nbr_send, nbr_recv,
-           stx_send, stx_recv, stz_send, stz_recv, los_send, los_recv, wide, own,
+           stx_send, stx_recv, stz_send, stz_recv,
+           lox_send, lox_recv, loz_send, loz_recv, los_send, los_recv, wide, own,
            rsx_send, rsx_recv, rsn_send, rsn_recv, rss_send, rss_recv, s_sem, r_sem):
     v = lax.axis_index("vocab")
     t = lax.axis_index("tok")
@@ -130,6 +126,8 @@
     found = jnp.sum(jnp.where(mine, 1.0, 0.0), axis=1, keepdims=True)
     block = jnp.sum(jnp.where(mine, jnp.broadcast_to(loc_row, (16, 256)), 0.0), axis=1, keepdims=True)
     odd = lax.rem(lax.broadcasted_iota(I32, (16, 1), 0), 2)
+    mapped = jnp.max(jnp.where((jnp.broadcast_to(own_row, (16, 256)) == v.astype(F32)) & (
+        jnp.broadcast_to(loc_row, (16, 256)) == row16.astype(F32)), 1.0, 0.0), axis=1, keepdims=True)
     first = jnp.where(found > 0.0, block.astype(I32) * 128 + odd, -4096)
     away = lax.broadcasted_iota(I32, (16, 2048), 1) - first
 
@@ -142,33 +140,29 @@
         send(AG1 + j - 1, mine_xt, mine_xt, at_z(4 * j))
 
     tl_copy.wait()
-
-    def pick1(g, c):
-        sel = jnp.concatenate([onehot(away == 2 * (8 * g + k)) for k in range(8)], axis=0)
-        send1[pl.ds(8 * g, 8)] = nt(sel, tl[...]).astype(BF).reshape(8, 16, 128)
-        return c
-
-    lax.fori_loop(0, 8, pick1, 0)
-
-    def spread1(i, c):
-        p = lax.rem(v + i, 64)
-        copy(A2A1, send1.at[p], recv1.at[v], (p, t)).start()
-        return c
-
-    lax.fori_loop(1, 64, spread1, 0)
-    pltpu.make_async_copy(send1.at[v], recv1.at[v], r_sem.at[A2A1]).start()
 
     top = tl[:, 0:128].astype(F32)
     for k in range(1, 16):
         top = jnp.maximum(top, tl[:, k * 128:(k + 1) * 128].astype(F32))
     top_col = jnp.max(top, axis=1, keepdims=True)
     total = jnp.zeros((128, 128), F32)
+    kept = jnp.zeros((128, 128), F32)
     for k in range(16):
-        total += jnp.exp(tl[:, k * 128:(k + 1) * 128].astype(F32) - top_col)
+        weight = jnp.exp(tl[:, k * 128:(k + 1) * 128].astype(F32) - top_col)
+        total += weight
+        kept += weight * mapped[k:k + 1, :]
     t_max = jnp.max(top.T, axis=0, keepdims=True)
     t_sum = jnp.sum(total.T, axis=0, keepdims=True)
-    lsx_send[...] = jnp.concatenate([t_max, t_sum, jnp.zeros((6, 128), F32)], axis=0)
+    t_kept = jnp.sum(kept.T, axis=0, keepdims=True)
+    lsx_send[...] = jnp.concatenate([t_max, t_sum, t_kept, jnp.zeros((5, 128), F32)], axis=0)
     lsx = [send(LSX + j - 1, lsx_send, lsx_recv.at[j - 1], at_x(j)) for j in range(1, 4)]
+
+    def pick1(g, c):
+        sel = jnp.concatenate([onehot(away == 2 * (8 * g + k)) for k in range(8)], axis=0)
+        send1[pl.ds(8 * g, 8)] = nt(sel, tl[...]).astype(BF).reshape(8, 16, 128)
+        return c
+
+    lax.fori_loop(0, 8, pick1, 0)
 
     def along_x(o):
         bb = lax.rem(b + o, 4)
@@ -186,9 +180,17 @@
     send(AG2 + 3, xt.at[pl.ds(2, 2), b, x], xt.at[pl.ds(2, 2), b, x], at_z(2))
     along_x(0)
 
+    def spread1(i, c):
+        p = lax.rem(v + i, 64)
+        copy(A2A1, send1.at[p], recv1.at[v], (p, t)).start()
+        return c
+
+    lax.fori_loop(1, 64, spread1, 0)
+    pltpu.make_async_copy(send1.at[v], recv1.at[v], r_sem.at[A2A1]).start()
+
     for c in lsx:
         c.wait_recv()
-    lsz_send[...] = combine_lse([lsx_send[...]] + [lsx_recv[j] for j in range(3)])
+    lsz_send[...] = combine_target([lsx_send[...]] + [lsx_recv[j] for j in range(3)])
     lsz = [send(LSZ + j - 1, lsz_send, lsz_recv.at[j - 1], at_z(j)) for j in range(1, 16)]
 
     r512 = lax.broadcasted_iota(I32, (512, 256), 0) // 2
@@ -214,17 +216,6 @@
     got_x(xt.at[pl.ds(2, 2), b_far, x], AG2 + 3, at_z(1))
     along_x(2)
 
-    pltpu.make_async_copy(recv1, recv1, r_sem.at[A2A1]).wait()
-    send2[...] = mm(pick_sel[...], recv1[...].reshape(1024, 128)).reshape(64, 8, 128).astype(BF)
-
-    def spread2(i, c):
-        p = lax.rem(v + i, 64)
-        copy(A2A2, send2.at[p], recv2.at[v], (p, t)).start()
-        return c
-
-    lax.fori_loop(1, 64, spread2, 0)
-    pltpu.make_async_copy(send2.at[v], recv2.at[v], r_sem.at[A2A2]).start()
-
     head_copy.wait()
     eye256 = onehot(sub == lane)
 
@@ -235,8 +226,30 @@
 
     lax.fori_loop(0, 16, turn, 0)
 
+    for c in lsz:
+        c.wait_recv()
+    stat = combine_target([lsz_send[...]] + [lsz_recv[j] for j in range(15)])
+    t_lse = stat[0:1] + jnp.log(stat[1:2])
+    t_mass = stat[2:3] * jnp.exp(stat[0:1] - t_lse)
+    lse_send[...] = jnp.concatenate([t_lse, t_mass, jnp.zeros((6, 128), F32)], axis=0)
+    lse_copy = send(LSN, lse_send, lse_recv, before)
+
+    def exchange_again():
+        pltpu.make_async_copy(recv1, recv1, r_sem.at[A2A1]).wait()
+        send2[...] = mm(pick_sel[...], recv1[...].reshape(1024, 128)).reshape(64, 8, 128).astype(BF)
+
+        def spread2(i, c):
+            p = lax.rem(v + i, 64)
+            copy(A2A2, send2.at[p], recv2.at[v], (p, t)).start()
+            return c
+
+        lax.fori_loop(1, 64, spread2, 0)
+        pltpu.make_async_copy(send2.at[v], recv2.at[v], r_sem.at[A2A2]).start()
+
     logits[...] = jnp.zeros((512, 256), F32)
     for o in (0, 3, 1, 2):
+        if o == 2:
+            exchange_again()
         bb = lax.rem(b + o, 4)
         for j in range(1, 4):
             ref = xt.at[:, bb, lax.rem(x + 4 - j, 4)]
@@ -249,11 +262,25 @@
 
         lax.fori_loop(0, 4, forward, 0)
 
-    for c in lsz:
-        c.wait_recv()
-    stat = combine_lse([lsz_send[...]] + [lsz_recv[j] for j in range(15)])
-    lse_send[...] = jnp.broadcast_to(stat[0:1] + jnp.log(stat[1:2]), (8, 128))
-    lse_copy = send(LSN, lse_send, lse_recv, before)
+    low = logits[...].astype(BF).astype(F32)
+    d_max = jnp.max(low, axis=0, keepdims=True)
+    d_sum = jnp.sum(jnp.exp(low - d_max), axis=0, keepdims=True)
+    stx_send[...] = jnp.concatenate([d_max[:, 0:128], d_max[:, 128:], d_sum[:, 0:128], d_sum[:, 128:]], axis=0)
+    stx = [send(STX + j - 1, stx_send, stx_recv.at[j - 1], at_x(j)) for j in range(1, 4)]
+    lse_copy.wait_recv()
+    l1 = lax.broadcasted_iota(I32, (1, 128), 1)
+
+    def with_next(k):
+        row = lse_send[k:k + 1, :]
+        late = jnp.where(l1 == 127, pltpu.roll(lse_recv[k:k + 1, :], 127, 1), pltpu.roll(row, 127, 1))
+        return jnp.concatenate([row, late], axis=1)
+
+    t_lse = with_next(0)
+    mass = with_next(1)
+    for c in stx:
+        c.wait_recv()
+    stz_send[...] = combine([stx_send[...]] + [stx_recv[j] for j in range(3)])
+    stz = [send(STZ + j - 1, stz_send, stz_recv.at[j - 1], at_z(j)) for j in range(1, 16)]
 
     pltpu.make_async_copy(recv2, recv2, r_sem.at[A2A2]).wait()
     picked = mm(place[...], recv2[...].reshape(512, 128)).astype(BF)
@@ -261,47 +288,25 @@
     l8 = lax.broadcasted_iota(I32, (8, 128), 1)
     nbr_send[...] = nt(onehot((r8 == 0) & (l8 == 0)), picked)
     nbr = send(NBR, nbr_send, nbr_recv, before)
-    low = logits[...].astype(BF).astype(F32)
-    d_max = jnp.max(low, axis=0, keepdims=True)
-    d_sum = jnp.sum(jnp.exp(low - d_max), axis=0, keepdims=True)
     sub128 = lax.broadcasted_iota(I32, (128, 128), 0)
     lane128 = lax.broadcasted_iota(I32, (128, 128), 1)
+    moved = mm(picked, onehot(sub128 == lane128 + 1))
     nbr.wait_recv()
-    moved = mm(picked, onehot(sub128 == lane128 + 1)) + lax.dot_general(
+    moved += lax.dot_general(
         nbr_recv[...].astype(BF), onehot((r8 == 0) & (l8 == 127)),
         (((0,), (0,)), ((), ())), preferred_element_type=F32)
-    picked2 = jnp.concatenate([picked.astype(F32), moved], axis=1)
-    lse_copy.wait_recv()
-    l1 = lax.broadcasted_iota(I32, (1, 128), 1)
-    t_lse = lse_send[0:1, :]
-    moved_lse = jnp.where(l1 == 127, pltpu.roll(lse_recv[0:1, :], 127, 1), pltpu.roll(t_lse, 127, 1))
-    probs[...] = jnp.exp(picked2 - jnp.concatenate([t_lse, moved_lse], axis=1))
-    mass = jnp.sum(probs[...], axis=0, keepdims=True)
-    term = jnp.sum(probs[...] * (d_max - low), axis=0, keepdims=True)
-    rows = []
-    for r in (d_max, d_sum, mass, term):
-        rows += [r[:, 0:128], r[:, 128:256]]
-    stx_send[...] = jnp.concatenate(rows, axis=0)
-    stx = [send(STX + j - 1, stx_send, stx_recv.at[j - 1], at_x(j)) for j in range(1, 4)]
-    for c in stx:
-        c.wait_recv()
-    stz_send[...] = jnp.concatenate(combine([stx_send[...]] + [stx_recv[j] for j in range(3)]), axis=0)
-    stz = [send(STZ + j - 1, stz_send, stz_recv.at[j - 1], at_z(j)) for j in range(1, 16)]
+    probs[...] = jnp.exp(jnp.concatenate([picked.astype(F32), moved], axis=1) - t_lse)
+
     for c in stz:
         c.wait_recv()
-    d_max, d_sum, mass, term = combine([stz_send[...]] + [stz_recv[j] for j in range(15)])
-    lift = jnp.log(d_sum)
-    d_lse = d_max + lift
-    loss = term + mass * lift
-    los_send[...] = jnp.concatenate([loss, jnp.zeros((6, 128), F32)], axis=0)
-    los = send(LOS, los_send, los_recv, after)
-
-    wide_row = lambda r: jnp.concatenate([r[0:1], r[1:2]], axis=1)
+    stat = combine([stz_send[...]] + [stz_recv[j] for j in range(15)])
+    d_lse = stat[0:2] + jnp.log(stat[2:4])
+
+    d_lse = jnp.concatenate([d_lse[0:1], d_lse[1:2]], axis=1)
     l256 = lax.broadcasted_iota(I32, (1, 256), 1)
     keep = jnp.where((l256 == 255) & (t == 7), 0.0, 64.0)
     low = logits[...].astype(BF).astype(F32)
-    grads = (keep * (wide_row(mass) * jnp.exp(low - wide_row(d_lse))
-                     - probs[...])).astype(BF)
+    grads = (keep * (mass * jnp.exp(low - d_lse) - probs[...])).astype(BF)
 
     def along_x_back(s, o):
         for j in range(1, 4):
@@ -325,6 +330,25 @@
         along_x_back(0, o)
     for o in (1, 3, 2, 0):
         along_x_back(1, o)
+
+    loss = jnp.sum(probs[...] * (d_lse - logits[...].astype(BF).astype(F32)), axis=0, keepdims=True)
+    lox_send[...] = jnp.concatenate([loss[:, 0:128], loss[:, 128:]], axis=0)
+    lox = [send(LOX + j - 1, lox_send, lox_recv.at[j - 1], at_x(j)) for j in range(1, 4)]
+
+    def loss_on():
+        for c in lox:
+            c.wait_recv()
+        loz_send[...] = lox_send[...] + lox_recv[0] + lox_recv[1] + lox_recv[2]
+        return [send(LOZ + j - 1, loz_send, loz_recv.at[j - 1], at_z(j)) for j in range(1, 16)]
+
+    def loss_over(loz):
+        for c in loz:
+            c.wait_recv()
+        whole = loz_send[...]
+        for j in range(15):
+            whole += loz_recv[j]
+        los_send[...] = jnp.concatenate([whole, jnp.zeros((6, 128), F32)], axis=0)
+        return send(LOS, los_send, los_recv, after)
 
     def summed(s, o, into):
         for j in range(1, 4):
@@ -365,12 +389,15 @@
         return [send(RSS + 3 * s + j - 1, rss_send.at[s, lax.rem(a + j, 4)], rss_recv.at[s, j - 1], at_z(4 * j))
                 for j in range(1, 4)]
 
-    for o in (1, 3, 2):
-        to_near(0, o)
+    to_near(0, 1)
+    to_near(0, 3)
+    loz = loss_on()
+    to_near(0, 2)
     summed(0, 0, rss_send.at[0])
     to_near(1, 1)
     far = to_far(0)
     to_near(1, 3)
+    los = loss_over(loz)
     to_near(1, 2)
     summed(1, 0, rss_send.at[1])
     far += to_far(1)
@@ -413,7 +440,8 @@
             v((64, 16, 128), BF), v((64, 16, 128), BF), v((64, 8, 128), BF), v((64, 8, 128), BF),
             v((512, 1024), BF), v((512, 512), BF), v((512, 256), F32), v((512, 256), F32),
             tile, v((3, 8, 128), F32), tile, v((15, 8, 128), F32), tile, tile, v((8, 512), F32), v((8, 512), F32),
-            tile, v((3, 8, 128), F32), tile, v((15, 8, 128), F32), tile, tile,
+            v((4, 128), F32), v((3, 4, 128), F32), v((4, 128), F32), v((15, 4, 128), F32),
+            v((2, 128), F32), v((3, 2, 128), F32), v((2, 128), F32), v((15, 2, 128), F32), tile, tile,
             v((4, 64, 256), F32), v((2, 4, 4, 64, 128), F32),
             v((2, 4, 4, 4, 64, 128), XT_DTYPE), v((2, 4, 3, 4, 64, 128), XT_DTYPE),
             v((2, 3, 4, 64, 128), F32), v((2, 3, 4, 64, 128), F32),

time: 123 us -> 130 us (1.057)
  the two profiles are of different devices: /device:TPU:1 before, /device:TPU:24 now
where the time goes in v3:
time: 130 us; the launch traced here: 129 us
  Pallas kernels  126 us (97%)
  local copies, waits for them, and re-layouts  2.6 us (2%)
    pallas_call x1, Pallas kernels, on_device(): pl.pallas_call(kernel, name='draft_loss', out_shape=(jax.ShapeDtypeStruct...  126 us
    unnamed x2, local copies, waits for them, and re-layouts  2.6 us

profile of v3, /device:TPU:24, one launch (start us, length us, event | category | flops | bytes accessed | tf_op | source)
XLA Modules:
  0.0 129.4 jit_solution(10826674255413684582)
XLA Ops:
  0.6 126.1 %draft_loss.1 = (bf16[2,64,128]{2,1,0:T(8,128)(2,1)}, f32[2,2]{1,0:T(2,128)}) custom-call(bf16[128,2048]{1,0:T(8,128)(2,1)} %tl_hbm.1, bf16[2,64,128]{2,1,0:T(8,128)(2,1)} %bitcast.4, bf16[512,4096]{1,0:T(8,128)(2,1)} %head_hbm.1, s32[1,256]{1,0:T(1,128)} %bitcast.5), custom_call_target="tpu_custom_call" | custom-call | flops 2147483648 | bytes 5242880 | tf_op jit(solution)/shard_map/draft_loss/pallas_call | solution.py:432
  126.8 1.4 %copy.8 = bf16[2,128,64]{1,2,0:T(8,128)(2,1)} copy(bf16[2,128,64]{1,2,0:T(8,128)(2,1)} %bitcast.3) | data formatting | bytes 65536
  128.1 1.2 copy.9

commit v4 on v3

--- a/solution.py
+++ b/solution.py
@@ -9,16 +9,15 @@
 F32 = jnp.float32
 I32 = jnp.int32
 MESH = pl.DeviceIdType.MESH
-XT_DTYPE = BF
 
 COUNTS = dict(AG1=3, A2A1=1, LSX=3, LSZ=15, LSN=1, AG2=4, AGX=12, A2A2=1, NBR=1, STX=3, STZ=15, LOX=3, LOZ=15, LOS=1,
-              RSX=24, RSN=8, RSS=6, HEAD=1, TL=1, HID=2, MAP=1)
+              RSX=12, RSN=4, RSZ=4, RSY=3, RSS=6, HEAD=1, TL=1, HID=2, MAP=1)
 BASE = {}
 N_SEMS = 0
 for _name, _count in COUNTS.items():
     BASE[_name] = N_SEMS
     N_SEMS += _count
-AG1, A2A1, LSX, LSZ, LSN, AG2, AGX, A2A2, NBR, STX, STZ, LOX, LOZ, LOS, RSX, RSN, RSS, HEAD, TL, HID, MAP = BASE.values()
+AG1, A2A1, LSX, LSZ, LSN, AG2, AGX, A2A2, NBR, STX, STZ, LOX, LOZ, LOS, RSX, RSN, RSZ, RSY, RSS, HEAD, TL, HID, MAP = BASE.values()
 
 
 def nt(a, b):
@@ -57,8 +56,8 @@
            bmap, tl, head, head_t, xt, send1, recv1, send2, recv2, pick_sel, place, logits, probs,
            lsx_send, lsx_recv, lsz_send, lsz_recv, lse_send, lse_recv, nbr_send, nbr_recv,
            stx_send, stx_recv, stz_send, stz_recv,
-           lox_send, lox_recv, loz_send, loz_recv, los_send, los_recv, wide, own,
-           rsx_send, rsx_recv, rsn_send, rsn_recv, rss_send, rss_recv, s_sem, r_sem):
+           lox_send, lox_recv, loz_send, loz_recv, los_send, los_recv, wide, own, own_z,
+           rsx_send, rsx_recv, rsn_send, rsn_recv, rsz_send, rsz_recv, rsy_recv, rss_send, rss_recv, s_sem, r_sem):
     v = lax.axis_index("vocab")
     t = lax.axis_index("tok")
     z = v // 4
@@ -141,28 +140,42 @@
 
     tl_copy.wait()
 
-    top = tl[:, 0:128].astype(F32)
-    for k in range(1, 16):
-        top = jnp.maximum(top, tl[:, k * 128:(k + 1) * 128].astype(F32))
-    top_col = jnp.max(top, axis=1, keepdims=True)
-    total = jnp.zeros((128, 128), F32)
-    kept = jnp.zeros((128, 128), F32)
-    for k in range(16):
-        weight = jnp.exp(tl[:, k * 128:(k + 1) * 128].astype(F32) - top_col)
-        total += weight
-        kept += weight * mapped[k:k + 1, :]
-    t_max = jnp.max(top.T, axis=0, keepdims=True)
-    t_sum = jnp.sum(total.T, axis=0, keepdims=True)
-    t_kept = jnp.sum(kept.T, axis=0, keepdims=True)
-    lsx_send[...] = jnp.concatenate([t_max, t_sum, t_kept, jnp.zeros((5, 128), F32)], axis=0)
-    lsx = [send(LSX + j - 1, lsx_send, lsx_recv.at[j - 1], at_x(j)) for j in range(1, 4)]
-
-    def pick1(g, c):
-        sel = jnp.concatenate([onehot(away == 2 * (8 * g + k)) for k in range(8)], axis=0)
-        send1[pl.ds(8 * g, 8)] = nt(sel, tl[...]).astype(BF).reshape(8, 16, 128)
-        return c
-
-    lax.fori_loop(0, 8, pick1, 0)
+    def targets():
+        top = tl[:, 0:128].astype(F32)
+        for k in range(1, 16):
+            top = jnp.maximum(top, tl[:, k * 128:(k + 1) * 128].astype(F32))
+        top_col = jnp.max(top, axis=1, keepdims=True)
+        total = jnp.zeros((128, 128), F32)
+        kept = jnp.zeros((128, 128), F32)
+        for k in range(16):
+            weight = jnp.exp(tl[:, k * 128:(k + 1) * 128].astype(F32) - top_col)
+            total += weight
+            kept += weight * mapped[k:k + 1, :]
+        t_max = jnp.max(top.T, axis=0, keepdims=True)
+        t_sum = jnp.sum(total.T, axis=0, keepdims=True)
+        t_kept = jnp.sum(kept.T, axis=0, keepdims=True)
+        lsx_send[...] = jnp.concatenate([t_max, t_sum, t_kept, jnp.zeros((5, 128), F32)], axis=0)
+        return [send(LSX + j - 1, lsx_send, lsx_recv.at[j - 1], at_x(j)) for j in range(1, 4)]
+
+    def picks():
+        def pick1(g, c):
+            sel = jnp.concatenate([onehot(away == 2 * (8 * g + k)) for k in range(8)], axis=0)
+            send1[pl.ds(8 * g, 8)] = nt(sel, tl[...]).astype(BF).reshape(8, 16, 128)
+            return c
+
+        lax.fori_loop(0, 8, pick1, 0)
+
+    def spread():
+        def spread1(i, c):
+            p = lax.rem(v + i, 64)
+            copy(A2A1, send1.at[p], recv1.at[v], (p, t)).start()
+            return c
+
+        lax.fori_loop(1, 64, spread1, 0)
+        pltpu.make_async_copy(send1.at[v], recv1.at[v], r_sem.at[A2A1]).start()
+
+    lsx = targets()
+    picks()
 
     def along_x(o):
         bb = lax.rem(b + o, 4)
@@ -179,14 +192,6 @@
     send(AG2 + 2, xt.at[pl.ds(0, 2), b, x], xt.at[pl.ds(0, 2), b, x], at_z(-2))
     send(AG2 + 3, xt.at[pl.ds(2, 2), b, x], xt.at[pl.ds(2, 2), b, x], at_z(2))
     along_x(0)
-
-    def spread1(i, c):
-        p = lax.rem(v + i, 64)
-        copy(A2A1, send1.at[p], recv1.at[v], (p, t)).start()
-        return c
-
-    lax.fori_loop(1, 64, spread1, 0)
-    pltpu.make_async_copy(send1.at[v], recv1.at[v], r_sem.at[A2A1]).start()
 
     for c in lsx:
         c.wait_recv()
@@ -215,6 +220,19 @@
     got_x(xt.at[pl.ds(0, 2), b_far, x], AG2 + 2, at_z(1))
     got_x(xt.at[pl.ds(2, 2), b_far, x], AG2 + 3, at_z(1))
     along_x(2)
+    spread()
+
+    def exchange_again():
+        pltpu.make_async_copy(recv1, recv1, r_sem.at[A2A1]).wait()
+        send2[...] = mm(pick_sel[...], recv1[...].reshape(1024, 128)).reshape(64, 8, 128).astype(BF)
+
+        def spread2(i, c):
+            p = lax.rem(v + i, 64)
+            copy(A2A2, send2.at[p], recv2.at[v], (p, t)).start()
+            return c
+
+        lax.fori_loop(1, 64, spread2, 0)
+        pltpu.make_async_copy(send2.at[v], recv2.at[v], r_sem.at[A2A2]).start()
 
     head_copy.wait()
     eye256 = onehot(sub == lane)
@@ -233,18 +251,6 @@
     t_mass = stat[2:3] * jnp.exp(stat[0:1] - t_lse)
     lse_send[...] = jnp.concatenate([t_lse, t_mass, jnp.zeros((6, 128), F32)], axis=0)
     lse_copy = send(LSN, lse_send, lse_recv, before)
-
-    def exchange_again():
-        pltpu.make_async_copy(recv1, recv1, r_sem.at[A2A1]).wait()
-        send2[...] = mm(pick_sel[...], recv1[...].reshape(1024, 128)).reshape(64, 8, 128).astype(BF)
-
-        def spread2(i, c):
-            p = lax.rem(v + i, 64)
-            copy(A2A2, send2.at[p], recv2.at[v], (p, t)).start()
-            return c
-
-        lax.fori_loop(1, 64, spread2, 0)
-        pltpu.make_async_copy(send2.at[v], recv2.at[v], r_sem.at[A2A2]).start()
 
     logits[...] = jnp.zeros((512, 256), F32)
     for o in (0, 3, 1, 2):
@@ -308,10 +314,15 @@
     low = logits[...].astype(BF).astype(F32)
     grads = (keep * (mass * jnp.exp(low - d_lse) - probs[...])).astype(BF)
 
-    def along_x_back(s, o):
+    loss = jnp.sum(probs[...] * (d_lse - logits[...].astype(BF).astype(F32)), axis=0, keepdims=True)
+    lox_send[...] = jnp.concatenate([loss[:, 0:128], loss[:, 128:]], axis=0)
+    lox = [send(LOX + j - 1, lox_send, lox_recv.at[j - 1], at_x(j)) for j in range(1, 4)]
+
+    def along_x_back(o):
         for j in range(1, 4):
-            send(RSX + 12 * s + 3 * o + j - 1, rsx_send.at[s, o, lax.rem(x + j, 4)], rsx_recv.at[s, o, j - 1], at_x(j))
-
+            send(RSX + 3 * o + j - 1, rsx_send.at[o, lax.rem(x + j, 4)], rsx_recv.at[o, j - 1], at_x(j))
+
+    first_z = []
     for o in (1, 3, 2, 0):
         bb = lax.rem(b + o, 4)
 
@@ -319,21 +330,24 @@
             cols = pl.ds(pl.multiple_of((i * 4 + bb) * 256, 256), 256)
             part = mm(head_t[cols, :], grads).reshape(4, 64, 256)
             wide[...] = part
-            for s in range(2):
-                half = slice(s * 128, (s + 1) * 128)
-                own[s, o, i] = wide[x, :, half]
-                for k in range(4):
-                    rsx_send[s, o, k, i] = part[k, :, half].astype(XT_DTYPE)
+            own[o, i] = wide[x, :, 0:128]
+            for k in range(4):
+                rsx_send[o, k, i] = part[k, :, 0:128].astype(BF)
+                if o == 0:
+                    own_z[k, i] = part[k, :, 128:256]
+                else:
+                    rsz_send[o - 1, k, i] = part[k, :, 128:256].astype(BF)
             return c
 
         lax.fori_loop(0, 4, backward, 0)
-        along_x_back(0, o)
-    for o in (1, 3, 2, 0):
-        along_x_back(1, o)
-
-    loss = jnp.sum(probs[...] * (d_lse - logits[...].astype(BF).astype(F32)), axis=0, keepdims=True)
-    lox_send[...] = jnp.concatenate([loss[:, 0:128], loss[:, 128:]], axis=0)
-    lox = [send(LOX + j - 1, lox_send, lox_recv.at[j - 1], at_x(j)) for j in range(1, 4)]
+        along_x_back(o)
+        if o == 1:
+            first_z.append(send(RSZ, rsz_send.at[0], rsz_recv.at[0], at_z(1)))
+        elif o == 3:
+            first_z.append(send(RSZ + 1, rsz_send.at[2], rsz_recv.at[2], at_z(-1)))
+        elif o == 2:
+            for k, part in ((0, pl.ds(0, 2)), (1, pl.ds(2, 2))):
+                first_z.append(send(RSZ + 2 + k, rsz_send.at[1, :, part], rsz_recv.at[1, :, part], at_z(4 * k - 2)))
 
     def loss_on():
         for c in lox:
@@ -350,57 +364,56 @@
         los_send[...] = jnp.concatenate([whole, jnp.zeros((6, 128), F32)], axis=0)
         return send(LOS, los_send, los_recv, after)
 
-    def summed(s, o, into):
+    def summed(o, into):
         for j in range(1, 4):
-            ref = rsx_recv.at[s, o, j - 1]
-            copy(RSX + 12 * s + 3 * o + j - 1, ref, ref, at_x(1)).wait_recv()
+            ref = rsx_recv.at[o, j - 1]
+            copy(RSX + 3 * o + j - 1, ref, ref, at_x(1)).wait_recv()
 
         def add(i, c):
-            into[i] = own[s, o, i] + rsx_recv[s, o, 0, i].astype(F32) + rsx_recv[s, o, 1, i].astype(F32) + rsx_recv[s, o, 2, i].astype(F32)
+            into[i] = own[o, i] + rsx_recv[o, 0, i].astype(F32) + rsx_recv[o, 1, i].astype(F32) + rsx_recv[o, 2, i].astype(F32)
             return c
 
         lax.fori_loop(0, 4, add, 0)
 
-    near = {0: [], 1: []}
-
-    def to_near(s, o):
-        k = RSN + 4 * s
-        if o == 1:
-            summed(s, o, rsn_send.at[s, 0])
-            near[s].append(send(k, rsn_send.at[s, 0], rsn_recv.at[s, 0], at_z(1)))
-        elif o == 3:
-            summed(s, o, rsn_send.at[s, 1])
-            near[s].append(send(k + 1, rsn_send.at[s, 1], rsn_recv.at[s, 1], at_z(-1)))
-        else:
-            summed(s, o, rsn_send.at[s, 2])
-            low2, high2 = pl.ds(0, 2), pl.ds(2, 2)
-            near[s].append(send(k + 2, rsn_send.at[s, 2, low2], rsn_recv.at[s, 2, low2], at_z(-2)))
-            near[s].append(send(k + 3, rsn_send.at[s, 2, high2], rsn_recv.at[s, 2, high2], at_z(2)))
-
-    def to_far(s):
-        for c in near[s]:
-            c.wait_recv()
-
-        def add_near(i, c):
-            rss_send[s, i] = rss_send[s, i] + rsn_recv[s, 0, i] + rsn_recv[s, 1, i] + rsn_recv[s, 2, i]
-            return c
-
-        lax.fori_loop(0, 4, add_near, 0)
+    def to_far(s, first, parts):
+        def add_last(i, c):
+            rss_send[s, i] = first(i) + parts[0, i] + parts[1, i] + parts[2, i]
+            return c
+
+        lax.fori_loop(0, 4, add_last, 0)
         return [send(RSS + 3 * s + j - 1, rss_send.at[s, lax.rem(a + j, 4)], rss_recv.at[s, j - 1], at_z(4 * j))
                 for j in range(1, 4)]
 
-    to_near(0, 1)
-    to_near(0, 3)
     loz = loss_on()
-    to_near(0, 2)
-    summed(0, 0, rss_send.at[0])
-    to_near(1, 1)
-    far = to_far(0)
-    to_near(1, 3)
+    near = []
+    for o in (1, 3, 2):
+        summed(o, rsn_send.at[o - 1])
+        if o == 1:
+            near.append(send(RSN, rsn_send.at[0], rsn_recv.at[0], at_z(1)))
+        elif o == 3:
+            near.append(send(RSN + 1, rsn_send.at[2], rsn_recv.at[2], at_z(-1)))
+        else:
+            for k, part in ((0, pl.ds(0, 2)), (1, pl.ds(2, 2))):
+                near.append(send(RSN + 2 + k, rsn_send.at[1, part], rsn_recv.at[1, part], at_z(4 * k - 2)))
+    for c in first_z:
+        c.wait_recv()
+
+    def add_z(i, c):
+        for k in range(4):
+            own_z[k, i] = (own_z[k, i] + rsz_recv[0, k, i].astype(F32) + rsz_recv[1, k, i].astype(F32)
+                           + rsz_recv[2, k, i].astype(F32))
+        return c
+
+    lax.fori_loop(0, 4, add_z, 0)
+    then_x = [send(RSY + j - 1, own_z.at[lax.rem(x + j, 4)], rsy_recv.at[j - 1], at_x(j)) for j in range(1, 4)]
+    summed(0, rss_send.at[0])
+    for c in near:
+        c.wait_recv()
+    far = to_far(0, lambda i: rss_send[0, i], rsn_recv)
     los = loss_over(loz)
-    to_near(1, 2)
-    summed(1, 0, rss_send.at[1])
-    far += to_far(1)
+    for c in then_x:
+        c.wait_recv()
+    far += to_far(1, lambda i: own_z[x, i], rsy_recv)
 
     los.wait_recv()
     here = los_send[...]
@@ -442,9 +455,10 @@
             tile, v((3, 8, 128), F32), tile, v((15, 8, 128), F32), tile, tile, v((8, 512), F32), v((8, 512), F32),
             v((4, 128), F32), v((3, 4, 128), F32), v((4, 128), F32), v((15, 4, 128), F32),
             v((2, 128), F32), v((3, 2, 128), F32), v((2, 128), F32), v((15, 2, 128), F32), tile, tile,
-            v((4, 64, 256), F32), v((2, 4, 4, 64, 128), F32),
-            v((2, 4, 4, 4, 64, 128), XT_DTYPE), v((2, 4, 3, 4, 64, 128), XT_DTYPE),
-            v((2, 3, 4, 64, 128), F32), v((2, 3, 4, 64, 128), F32),
+            v((4, 64, 256), F32), v((4, 4, 64, 128), F32), v((4, 4, 64, 128), F32),
+            v((4, 4, 4, 64, 128), BF), v((4, 3, 4, 64, 128), BF),
+            v((3, 4, 64, 128), F32), v((3, 4, 64, 128), F32),
+            v((3, 4, 4, 64, 128), BF), v((3, 4, 4, 64, 128), BF), v((3, 4, 64, 128), F32),
             v((2, 4, 64, 128), F32), v((2, 3, 64, 128), F32),
             pltpu.SemaphoreType.DMA((N_SEMS,)), pltpu.SemaphoreType.DMA((N_SEMS,)),
         ],

time: 130 us -> 112 us (0.86)
  the two profiles are of different devices: /device:TPU:24 before, /device:TPU:1 now
where the time goes in v4:
time: 112 us; the launch traced here: 111 us
  Pallas kernels  108 us (96%)
  local copies, waits for them, and re-layouts  2.6 us (2%)
    pallas_call x1, Pallas kernels, on_device(): pl.pallas_call(kernel, name='draft_loss', out_shape=(jax.ShapeDtypeStruct...  108 us
    unnamed x2, local copies, waits for them, and re-layouts  2.6 us

profile of v4, /device:TPU:1, one launch (start us, length us, event | category | flops | bytes accessed | tf_op | source)
XLA Modules:
  0.0 111.2 jit_solution(17397653936417663806)
XLA Ops:
  0.6 108.0 %draft_loss.1 = (bf16[2,64,128]{2,1,0:T(8,128)(2,1)}, f32[2,2]{1,0:T(2,128)}) custom-call(bf16[128,2048]{1,0:T(8,128)(2,1)} %tl_hbm.1, bf16[2,64,128]{2,1,0:T(8,128)(2,1)} %bitcast.4, bf16[512,4096]{1,0:T(8,128)(2,1)} %head_hbm.1, s32[1,256]{1,0:T(1,128)} %bitcast.5), custom_call_target="tpu_custom_call" | custom-call | flops 2147483648 | bytes 5242880 | tf_op jit(solution)/shard_map/draft_loss/pallas_call | solution.py:445
  108.6 1.4 %copy.8 = bf16[2,128,64]{1,2,0:T(8,128)(2,1)} copy(bf16[2,128,64]{1,2,0:T(8,128)(2,1)} %bitcast.3) | data formatting | bytes 65536
  110.0 1.2 %copy.9 = f32[2,2]{1,0:T(2,128)} copy(f32[2,2]{1,0:T(2,128)} %get-tuple-element.9) | data formatting | bytes 32

commit v5 on v4

--- a/solution.py
+++ b/solution.py
@@ -57,7 +57,7 @@
            lsx_send, lsx_recv, lsz_send, lsz_recv, lse_send, lse_recv, nbr_send, nbr_recv,
            stx_send, stx_recv, stz_send, stz_recv,
            lox_send, lox_recv, loz_send, loz_recv, los_send, los_recv, wide, own, own_z,
-           rsx_send, rsx_recv, rsn_send, rsn_recv, rsz_send, rsz_recv, rsy_recv, rss_send, rss_recv, s_sem, r_sem):
+           rsx_send, rsx_recv, rsn_send, rsn_recv, rsz_send, rsz_recv, rsy_recv, rss_send, far_send, rss_recv, s_sem, r_sem):
     v = lax.axis_index("vocab")
     t = lax.axis_index("tok")
     z = v // 4
@@ -130,16 +130,6 @@
     first = jnp.where(found > 0.0, block.astype(I32) * 128 + odd, -4096)
     away = lax.broadcasted_iota(I32, (16, 2048), 1) - first
 
-    for c in hid_copies:
-        c.wait()
-    pl.semaphore_wait(barrier, 65)
-
-    for j in range(1, 4):
-        mine_xt = xt.at[a, b, x]
-        send(AG1 + j - 1, mine_xt, mine_xt, at_z(4 * j))
-
-    tl_copy.wait()
-
     def targets():
         top = tl[:, 0:128].astype(F32)
         for k in range(1, 16):
@@ -155,6 +145,7 @@
         t_sum = jnp.sum(total.T, axis=0, keepdims=True)
         t_kept = jnp.sum(kept.T, axis=0, keepdims=True)
         lsx_send[...] = jnp.concatenate([t_max, t_sum, t_kept, jnp.zeros((5, 128), F32)], axis=0)
+    def targets_send():
         return [send(LSX + j - 1, lsx_send, lsx_recv.at[j - 1], at_x(j)) for j in range(1, 4)]
 
     def picks():
@@ -165,6 +156,14 @@
 
         lax.fori_loop(0, 8, pick1, 0)
 
+    for c in hid_copies:
+        c.wait()
+    pl.semaphore_wait(barrier, 65)
+
+    for j in range(1, 4):
+        mine_xt = xt.at[a, b, x]
+        send(AG1 + j - 1, mine_xt, mine_xt, at_z(4 * j))
+
     def spread():
         def spread1(i, c):
             p = lax.rem(v + i, 64)
@@ -174,8 +173,13 @@
         lax.fori_loop(1, 64, spread1, 0)
         pltpu.make_async_copy(send1.at[v], recv1.at[v], r_sem.at[A2A1]).start()
 
-    lsx = targets()
+    tl_copy.wait()
+    targets()
+    lsx = targets_send()
     picks()
+
+    def got_x(ref_of, k, dev):
+        copy(k, ref_of, ref_of, dev).wait_recv()
 
     def along_x(o):
         bb = lax.rem(b + o, 4)
@@ -206,9 +210,6 @@
     rr = lax.broadcasted_iota(I32, (512, 1), 0)
     goes = (lax.rem(rr, 128) // 2) * 8 + (rr // 128) * 2 + lax.rem(rr, 2)
     place[...] = onehot(lax.broadcasted_iota(I32, (512, 512), 1) == goes)
-
-    def got_x(ref_of, k, dev):
-        copy(k, ref_of, ref_of, dev).wait_recv()
 
     b_prev = lax.rem(b + 3, 4)
     b_next = lax.rem(b + 1, 4)
@@ -221,7 +222,6 @@
     got_x(xt.at[pl.ds(2, 2), b_far, x], AG2 + 3, at_z(1))
     along_x(2)
     spread()
-
     def exchange_again():
         pltpu.make_async_copy(recv1, recv1, r_sem.at[A2A1]).wait()
         send2[...] = mm(pick_sel[...], recv1[...].reshape(1024, 128)).reshape(64, 8, 128).astype(BF)
@@ -243,14 +243,6 @@
         return c
 
     lax.fori_loop(0, 16, turn, 0)
-
-    for c in lsz:
-        c.wait_recv()
-    stat = combine_target([lsz_send[...]] + [lsz_recv[j] for j in range(15)])
-    t_lse = stat[0:1] + jnp.log(stat[1:2])
-    t_mass = stat[2:3] * jnp.exp(stat[0:1] - t_lse)
-    lse_send[...] = jnp.concatenate([t_lse, t_mass, jnp.zeros((6, 128), F32)], axis=0)
-    lse_copy = send(LSN, lse_send, lse_recv, before)
 
     logits[...] = jnp.zeros((512, 256), F32)
     for o in (0, 3, 1, 2):
@@ -273,16 +265,14 @@
     d_sum = jnp.sum(jnp.exp(low - d_max), axis=0, keepdims=True)
     stx_send[...] = jnp.concatenate([d_max[:, 0:128], d_max[:, 128:], d_sum[:, 0:128], d_sum[:, 128:]], axis=0)
     stx = [send(STX + j - 1, stx_send, stx_recv.at[j - 1], at_x(j)) for j in range(1, 4)]
-    lse_copy.wait_recv()
-    l1 = lax.broadcasted_iota(I32, (1, 128), 1)
-
-    def with_next(k):
-        row = lse_send[k:k + 1, :]
-        late = jnp.where(l1 == 127, pltpu.roll(lse_recv[k:k + 1, :], 127, 1), pltpu.roll(row, 127, 1))
-        return jnp.concatenate([row, late], axis=1)
-
-    t_lse = with_next(0)
-    mass = with_next(1)
+    for c in lsz:
+        c.wait_recv()
+    stat = combine_target([lsz_send[...]] + [lsz_recv[j] for j in range(15)])
+    t_lse = stat[0:1] + jnp.log(stat[1:2])
+    t_mass = stat[2:3] * jnp.exp(stat[0:1] - t_lse)
+    lse_send[...] = jnp.concatenate([t_lse, t_mass, jnp.zeros((6, 128), F32)], axis=0)
+    lse_copy = send(LSN, lse_send, lse_recv, before)
+
     for c in stx:
         c.wait_recv()
     stz_send[...] = combine([stx_send[...]] + [stx_recv[j] for j in range(3)])
@@ -301,6 +291,16 @@
     moved += lax.dot_general(
         nbr_recv[...].astype(BF), onehot((r8 == 0) & (l8 == 127)),
         (((0,), (0,)), ((), ())), preferred_element_type=F32)
+    lse_copy.wait_recv()
+    l1 = lax.broadcasted_iota(I32, (1, 128), 1)
+
+    def with_next(k):
+        row = lse_send[k:k + 1, :]
+        late = jnp.where(l1 == 127, pltpu.roll(lse_recv[k:k + 1, :], 127, 1), pltpu.roll(row, 127, 1))
+        return jnp.concatenate([row, late], axis=1)
+
+    t_lse = with_next(0)
+    mass = with_next(1)
     probs[...] = jnp.exp(jnp.concatenate([picked.astype(F32), moved], axis=1) - t_lse)
 
     for c in stz:
@@ -363,7 +363,6 @@
             whole += loz_recv[j]
         los_send[...] = jnp.concatenate([whole, jnp.zeros((6, 128), F32)], axis=0)
         return send(LOS, los_send, los_recv, after)
-
     def summed(o, into):
         for j in range(1, 4):
             ref = rsx_recv.at[o, j - 1]
@@ -381,7 +380,12 @@
             return c
 
         lax.fori_loop(0, 4, add_last, 0)
-        return [send(RSS + 3 * s + j - 1, rss_send.at[s, lax.rem(a + j, 4)], rss_recv.at[s, j - 1], at_z(4 * j))
+        def narrow(i, c):
+            far_send[s, i] = rss_send[s, i].astype(BF)
+            return c
+
+        lax.fori_loop(0, 4, narrow, 0)
+        return [send(RSS + 3 * s + j - 1, far_send.at[s, lax.rem(a + j, 4)], rss_recv.at[s, j - 1], at_z(4 * j))
                 for j in range(1, 4)]
 
     loz = loss_on()
@@ -428,7 +432,7 @@
     for c in far:
         c.wait_recv()
     for s in range(2):
-        grad_out[s] = (rss_send[s, a] + rss_recv[s, 0] + rss_recv[s, 1] + rss_recv[s, 2]).astype(BF)
+        grad_out[s] = (rss_send[s, a] + rss_recv[s, 0].astype(F32) + rss_recv[s, 1].astype(F32) + rss_recv[s, 2].astype(F32)).astype(BF)
 
     for c in sent:
         c.wait_send()
@@ -459,7 +463,7 @@
             v((4, 4, 4, 64, 128), BF), v((4, 3, 4, 64, 128), BF),
             v((3, 4, 64, 128), F32), v((3, 4, 64, 128), F32),
             v((3, 4, 4, 64, 128), BF), v((3, 4, 4, 64, 128), BF), v((3, 4, 64, 128), F32),
-            v((2, 4, 64, 128), F32), v((2, 3, 64, 128), F32),
+            v((2, 4, 64, 128), F32), v((2, 4, 64, 128), BF), v((2, 3, 64, 128), BF),
             pltpu.SemaphoreType.DMA((N_SEMS,)), pltpu.SemaphoreType.DMA((N_SEMS,)),
         ],
         compiler_params=pltpu.CompilerParams(

time: 112 us -> 106 us (0.946)
  Pallas kernels: 108 us -> 103 us
    pallas_call x1, Pallas kernels: 108 us -> 103 us  [on_device(): pl.pallas_call(kernel, name='draft_loss', out_shape=(jax.ShapeDtypeStruct...]
where the time goes in v5:
time: 106 us
  Pallas kernels  103 us (97%)
  local copies, waits for them, and re-layouts  2.6 us (2%)
    pallas_call x1, Pallas kernels, on_device(): pl.pallas_call(kernel, name='draft_loss', out_shape=(jax.ShapeDtypeStruct...  103 us
    unnamed x2, local copies, waits for them, and re-layouts  2.6 us

profile of v5, /device:TPU:1, one launch (start us, length us, event | category | flops | bytes accessed | tf_op | source)
XLA Modules:
  0.0 106.0 jit_solution(3090594321994403082)
XLA Ops:
  0.6 102.8 %draft_loss.1 = (bf16[2,64,128]{2,1,0:T(8,128)(2,1)}, f32[2,2]{1,0:T(2,128)}) custom-call(bf16[128,2048]{1,0:T(8,128)(2,1)} %tl_hbm.1, bf16[2,64,128]{2,1,0:T(8,128)(2,1)} %bitcast.4, bf16[512,4096]{1,0:T(8,128)(2,1)} %head_hbm.1, s32[1,256]{1,0:T(1,128)} %bitcast.5), custom_call_target="tpu_custom_call" | custom-call | flops 2147483648 | bytes 5242880 | tf_op jit(solution)/shard_map/draft_loss/pallas_call | solution.py:449
  103.4 1.4 %copy.8 = bf16[2,128,64]{1,2,0:T(8,128)(2,1)} copy(bf16[2,128,64]{1,2,0:T(8,128)(2,1)} %bitcast.3) | data formatting | bytes 65536
  104.8 1.2 %copy.9 = f32[2,2]{1,0:T(2,128)} copy(f32[2,2]{1,0:T(2,128)} %get-tuple-element.9) | data formatting | bytes 32

commit v6 on v5

--- a/solution.py
+++ b/solution.py
@@ -196,6 +196,7 @@
     send(AG2 + 2, xt.at[pl.ds(0, 2), b, x], xt.at[pl.ds(0, 2), b, x], at_z(-2))
     send(AG2 + 3, xt.at[pl.ds(2, 2), b, x], xt.at[pl.ds(2, 2), b, x], at_z(2))
     along_x(0)
+    spread()
 
     for c in lsx:
         c.wait_recv()
@@ -221,7 +222,6 @@
     got_x(xt.at[pl.ds(0, 2), b_far, x], AG2 + 2, at_z(1))
     got_x(xt.at[pl.ds(2, 2), b_far, x], AG2 + 3, at_z(1))
     along_x(2)
-    spread()
     def exchange_again():
         pltpu.make_async_copy(recv1, recv1, r_sem.at[A2A1]).wait()
         send2[...] = mm(pick_sel[...], recv1[...].reshape(1024, 128)).reshape(64, 8, 128).astype(BF)
@@ -340,7 +340,6 @@
             return c
 
         lax.fori_loop(0, 4, backward, 0)
-        along_x_back(o)
         if o == 1:
             first_z.append(send(RSZ, rsz_send.at[0], rsz_recv.at[0], at_z(1)))
         elif o == 3:
@@ -348,6 +347,7 @@
         elif o == 2:
             for k, part in ((0, pl.ds(0, 2)), (1, pl.ds(2, 2))):
                 first_z.append(send(RSZ + 2 + k, rsz_send.at[1, :, part], rsz_recv.at[1, :, part], at_z(4 * k - 2)))
+        along_x_back(o)
 
     def loss_on():
         for c in lox:
@@ -374,6 +374,11 @@
 
         lax.fori_loop(0, 4, add, 0)
 
+    def far_copy(s, k):
+        i = k + jnp.where(a <= k, 1, 0)
+        j = lax.rem(i + 4 - a, 4)
+        return send(RSS + 3 * s + j - 1, far_send.at[s, i], rss_recv.at[s, j - 1], ((i * 4 + b) * 4 + x, t))
+
     def to_far(s, first, parts):
         def add_last(i, c):
             rss_send[s, i] = first(i) + parts[0, i] + parts[1, i] + parts[2, i]
@@ -385,8 +390,7 @@
             return c
 
         lax.fori_loop(0, 4, narrow, 0)
-        return [send(RSS + 3 * s + j - 1, far_send.at[s, lax.rem(a + j, 4)], rss_recv.at[s, j - 1], at_z(4 * j))
-                for j in range(1, 4)]
+        return [far_copy(s, k) for k in range(3)]
 
     loz = loss_on()
     near = []

time: 106 us -> 106 us (level); the launches traced: 106 us -> 105 us
  Pallas kernels: 103 us -> 101 us
    pallas_call x1, Pallas kernels: 103 us -> 101 us  [on_device(): pl.pallas_call(kernel, name='draft_loss', out_shape=(jax.ShapeDtypeStruct...]
where the time goes in v6:
time: 106 us; the launch traced here: 105 us
  Pallas kernels  101 us (95%)
  local copies, waits for them, and re-layouts  2.6 us (2%)
    pallas_call x1, Pallas kernels, on_device(): pl.pallas_call(kernel, name='draft_loss', out_shape=(jax.ShapeDtypeStruct...  101 us
    unnamed x2, local copies, waits for them, and re-layouts  2.6 us

profile of v6, /device:TPU:1, one launch (start us, length us, event | category | flops | bytes accessed | tf_op | source)
XLA Modules:
  0.0 104.6 jit_solution(10925304143562601069)
XLA Ops:
  0.6 101.3 %draft_loss.1 = (bf16[2,64,128]{2,1,0:T(8,128)(2,1)}, f32[2,2]{1,0:T(2,128)}) custom-call(bf16[128,2048]{1,0:T(8,128)(2,1)} %tl_hbm.1, bf16[2,64,128]{2,1,0:T(8,128)(2,1)} %bitcast.4, bf16[512,4096]{1,0:T(8,128)(2,1)} %head_hbm.1, s32[1,256]{1,0:T(1,128)} %bitcast.5), custom_call_target="tpu_custom_call" | custom-call | flops 2147483648 | bytes 5242880 | tf_op jit(solution)/shard_map/draft_loss/pallas_call | solution.py:453
  102.0 1.4 %copy.8 = bf16[2,128,64]{1,2,0:T(8,128)(2,1)} copy(bf16[2,128,64]{1,2,0:T(8,128)(2,1)} %bitcast.3) | data formatting | bytes 65536
  103.3 1.2 %copy.9 = f32[2,2]{1,0:T(2,128)} copy(f32[2,2]{1,0:T(2,128)} %get-tuple-element.9) | data formatting | bytes 32

commit v7 on v6

--- a/solution.py
+++ b/solution.py
@@ -78,6 +78,10 @@
         return pltpu.make_async_remote_copy(
             src_ref=src, dst_ref=dst, send_sem=s_sem.at[k], recv_sem=r_sem.at[k],
             device_id=dev, device_id_type=MESH)
+
+    def both_ways(i):
+        half = i // 2
+        return lax.rem(v + jnp.where(i - 2 * half == 1, half + 1, 64 - half), 64)
 
     sent = []
 
@@ -166,7 +170,7 @@
 
     def spread():
         def spread1(i, c):
-            p = lax.rem(v + i, 64)
+            p = both_ways(i)
             copy(A2A1, send1.at[p], recv1.at[v], (p, t)).start()
             return c
 
@@ -227,7 +231,7 @@
         send2[...] = mm(pick_sel[...], recv1[...].reshape(1024, 128)).reshape(64, 8, 128).astype(BF)
 
         def spread2(i, c):
-            p = lax.rem(v + i, 64)
+            p = both_ways(i)
             copy(A2A2, send2.at[p], recv2.at[v], (p, t)).start()
             return c
 

time: 106 us -> 105 us (level); the launches traced: 105 us -> 105 us
  no operation moved by 1% of the time
where the time goes in v7:
time: 105 us
  Pallas kernels  102 us (97%)
  local copies, waits for them, and re-layouts  2.6 us (2%)
    pallas_call x1, Pallas kernels, on_device(): pl.pallas_call(kernel, name='draft_loss', out_shape=(jax.ShapeDtypeStruct...  102 us
    unnamed x2, local copies, waits for them, and re-layouts  2.6 us

profile of v7, /device:TPU:1, one launch (start us, length us, event | category | flops | bytes accessed | tf_op | source)
XLA Modules:
  0.0 105.1 jit_solution(16784558679834467538)
XLA Ops:
  0.6 101.9 %draft_loss.1 = (bf16[2,64,128]{2,1,0:T(8,128)(2,1)}, f32[2,2]{1,0:T(2,128)}) custom-call(bf16[128,2048]{1,0:T(8,128)(2,1)} %tl_hbm.1, bf16[2,64,128]{2,1,0:T(8,128)(2,1)} %bitcast.4, bf16[512,4096]{1,0:T(8,128)(2,1)} %head_hbm.1, s32[1,256]{1,0:T(1,128)} %bitcast.5), custom_call_target="tpu_custom_call" | custom-call | flops 2147483648 | bytes 5242880 | tf_op jit(solution)/shard_map/draft_loss/pallas_call | solution.py:457
  102.5 1.4 %copy.8 = bf16[2,128,64]{1,2,0:T(8,128)(2,1)} copy(bf16[2,128,64]{1,2,0:T(8,128)(2,1)} %bitcast.3) | data formatting | bytes 65536
  103.9 1.2 %copy.9 = f32[2,2]{1,0:T(2,128)} copy(f32[2,2]{1,0:T(2,128)} %get-tuple-element.9) | data formatting | bytes 32
